TPU v7x, 128 devices: a whole 4x4x4 slice. The times are simulated.
128 devices in a mesh: leaf: 32 (over x_lo, y, z), blk: 4 (over x_hi, core).
Axes of the slice: x: 4 (x_hi: 2, x_lo: 2; x = x_hi * 2 + x_lo), y: 4, z: 4, core: 2. Of those that a mesh axis runs over, the one named last changes fastest.
Arguments:
- stiffness: bfloat16 [64, 2048, 2048], P('leaf', 'blk'), may hold values from -6 to 6
- modes: bfloat16 [64, 2048, 512], P('leaf', 'blk'), may hold values from -0.125 to 0.125
- basis: bfloat16 [16384, 2048], P('leaf', 'blk'), may hold values from -0.125 to 0.125
- eigen: float32 [64, 512], P('leaf'), may hold values from 20 to 200
- counts: int32 [64], P('leaf'), may hold values from 80 to 400
- ancestry: int32 [64], P('leaf'), may hold values from 0 to 7
Outputs:
- projection: bfloat16 [64, 512, 2048], P('leaf', None, 'blk')
- correction: float32 [16384, 2048], P('leaf', 'blk')
All inputs are finite; a program needn't handle non-finite values.
Results may differ from a plain program's by a relative error of at most 0.018.
Values may be sent and summed in bfloat16 or wider, within the bound.
No kernel may reach another device: no remote copies, remote signals or barrier semaphores. Data moves between devices by JAX's collectives and lax.ppermute only.
A program may use at most 192 MiB of HBM per device.

v0:
```python
import jax
import jax.numpy as jnp
import numpy as np
from jax import lax
from jax.experimental import pallas as pl
from jax.experimental.pallas import tpu as pltpu
from jax.sharding import PartitionSpec as P

AXES = ("leaf", "blk")
SHAPE = (2, 4, 4, 2, 2)
ROWS = 400
LINES = 416
SPARE = 416
TILE = 512
WIDTHS = (256, 256)
ORDER = (2, 1, 3, 0)
BF = jnp.bfloat16
F32 = jnp.float32
VMEM = pl.BlockSpec(memory_space=pltpu.VMEM)
SMEM = pl.BlockSpec(memory_space=pltpu.SMEM)
HBM = pl.BlockSpec(memory_space=pltpu.HBM)
ANY = pl.BlockSpec(memory_space=pl.ANY)


def shift(value, xl=0, y=0, z=0, xh=0, c=0):
    pairs = []
    for spot in np.ndindex(*SHAPE):
        to = tuple((a + b) % n for a, b, n in zip(spot, (xl, y, z, xh, c), SHAPE))
        pairs.append((int(np.ravel_multi_index(spot, SHAPE)), int(np.ravel_multi_index(to, SHAPE))))
    return lax.ppermute(value, AXES, pairs)


def tdot(a, b):
    return lax.dot_general(a, b, (((0,), (0,)), ((), ())), preferred_element_type=F32)


def couple(which, spot, modes, stiffness):
    def kernel(spot, modes, stiffness, *outs):
        sub = spot[3] ^ which
        tag = jnp.zeros((LINES - ROWS, TILE), F32)
        if which == 0:
            places = [relative(spot[6 + (spot[3] ^ j)], spot) for j in range(2)]
            tag = tag + (places[0] + 8 * places[1]).astype(F32)
        live = lax.broadcasted_iota(jnp.int32, (ROWS, TILE), 0) < spot[4 + sub]
        turned = modes[sub].astype(F32).T[:ROWS].astype(BF)
        for k, d in enumerate(ORDER):
            first = pl.multiple_of(((spot[2] + d) & 3) * TILE, TILE)
            value = jnp.dot(turned, stiffness[sub, :, pl.ds(first, TILE)], preferred_element_type=F32)
            outs[k][0, pl.ds(0, ROWS)] = jnp.where(live, value, 0.0).astype(BF)
            outs[k][0, pl.ds(ROWS, LINES - ROWS)] = tag.astype(BF)

    return pl.pallas_call(
        kernel,
        out_shape=[jax.ShapeDtypeStruct((1, LINES, TILE), BF)] * 4,
        in_specs=[SMEM] + [VMEM] * 2,
        out_specs=[VMEM] * 4,
        compiler_params=pltpu.CompilerParams(vmem_limit_bytes=20 << 20),
        cost_estimate=pl.CostEstimate(flops=1 << 10, bytes_accessed=1 << 10, transcendentals=0),
        name="couple",
    )(spot, modes, stiffness)


def relative(separator, spot):
    return ((separator >> 2) ^ spot[0]) * 4 + ((separator - spot[1]) & 3)


def tag_of(own):
    return own[pl.ds(ROWS, 8), pl.ds(0, 128)].astype(F32)


def places_of(own):
    both = (jnp.max(tag_of(own)) * 0.5).astype(jnp.int32)
    return both & 7, both >> 3


def halves(value):
    first, out = 0, []
    for width in WIDTHS:
        out.append(value[..., first : first + width])
        first += width
    return out


def project(sides, tiles, carry=(), whole=False):
    count = len(sides)
    slots = [slot for slot, _ in carry]

    def kernel(*refs):
        sides, tiles = refs[: 2 * count], refs[2 * count : 2 * count + 8]
        carried = refs[2 * count + 8 : 2 * count + 8 + len(slots)]
        outs, (held, sems) = refs[2 * count + 8 + len(slots) : -2], refs[-2:]
        for n in range(count):
            for j, place in enumerate(places_of(sides[2 * n])):
                for k in range(8):

                    @pl.when(place == k)
                    def _():
                        pltpu.make_async_copy(tiles[k], held.at[2 * n + j], sems.at[2 * n + j]).start()

        for n in range(2 * count):
            pltpu.make_async_copy(tiles[0], held.at[n], sems.at[n]).wait()
            value = jnp.dot(sides[n][pl.ds(0, ROWS)], held[n], preferred_element_type=F32)
            if slots and slots[n // 2] == n % 2:
                value = value + carried[n // 2][0, pl.ds(0, ROWS)].astype(F32)
            if whole:
                outs[n][0, pl.ds(0, ROWS)] = value.astype(BF)
                outs[n][0, pl.ds(ROWS, SPARE - ROWS)] = jnp.zeros((SPARE - ROWS, TILE), BF)
                continue
            for h, half in enumerate(halves(value)):
                outs[n // 2 * len(WIDTHS) + h][n % 2] = half.astype(BF)

    shapes = [(1, SPARE, TILE)] * 2 if whole else [(2, ROWS, width) for width in WIDTHS] * count
    flat = pl.pallas_call(
        kernel,
        out_shape=[jax.ShapeDtypeStruct(shape, BF) for shape in shapes],
        in_specs=[VMEM] * (2 * count) + [ANY] * 8 + [VMEM] * len(slots),
        out_specs=[VMEM] * len(shapes),
        scratch_shapes=[pltpu.VMEM((2 * count, TILE, TILE), BF), pltpu.SemaphoreType.DMA((2 * count,))],
        compiler_params=pltpu.CompilerParams(vmem_limit_bytes=12 << 20),
        cost_estimate=pl.CostEstimate(flops=1 << 10, bytes_accessed=1 << 10, transcendentals=0),
        name="project",
    )(*[item for pair in sides for item in pair], *tiles, *[item for _, item in carry])
    if whole:
        return flat
    return [flat[n * len(WIDTHS) : (n + 1) * len(WIDTHS)] for n in range(count)]


def scale(eigen, parts):
    def kernel(eigen, first, second, third, total, scaled):
        for j in range(2):
            value = first[j].astype(F32) + second[j].astype(F32) + third[j].astype(F32)
            total[j] = value.astype(BF)
            scaled[j] = (value * (1.0 / eigen[j, pl.ds(0, ROWS)])).astype(BF)

    return pl.pallas_call(
        kernel,
        out_shape=[jax.ShapeDtypeStruct(parts[0].shape, BF)] * 2,
        in_specs=[VMEM] * 4,
        out_specs=[VMEM] * 2,
        compiler_params=pltpu.CompilerParams(vmem_limit_bytes=10 << 20),
        cost_estimate=pl.CostEstimate(flops=1 << 10, bytes_accessed=1 << 10, transcendentals=0),
        name="scale",
    )(eigen, *parts)


def correct(coupled, scaled):
    width = scaled[0].shape[2]

    def kernel(*refs):
        coupled, scaled, outs, total = refs[:8], refs[8:-5], refs[-5:-1], refs[-1]
        scaled = [ref.at[j] for ref in scaled for j in range(ref.shape[0])]
        total[...] = jnp.zeros_like(total)
        tags = sum(tag_of(coupled[2 * d]) * (0.5 * 64**d) for d in range(4))
        places = jnp.max(tags).astype(jnp.int32)
        for d in range(4):
            for j in range(2):
                place = (places >> (6 * d + 3 * j)) & 7
                total[place] += tdot(coupled[2 * d + j][pl.ds(0, ROWS)], scaled[2 * d + j][...])
        for k in range(8):
            outs[k % 4][k // 4] = total[k].astype(BF)

    return pl.pallas_call(
        kernel,
        out_shape=[jax.ShapeDtypeStruct((2, TILE, width), BF)] * 4,
        in_specs=[VMEM] * (8 + len(scaled)),
        out_specs=[VMEM] * 4,
        scratch_shapes=[pltpu.VMEM((8, TILE, width), F32)],
        compiler_params=pltpu.CompilerParams(vmem_limit_bytes=20 << 20),
        cost_estimate=pl.CostEstimate(flops=1 << 10, bytes_accessed=1 << 10, transcendentals=0),
        name="correct",
    )(*coupled, *scaled)


def add(a, b):
    return (a.astype(F32) + b.astype(F32)).astype(BF)


def per_device(stiffness, modes, basis, eigen, counts, ancestry):
    leaf, blk = lax.axis_index("leaf"), lax.axis_index("blk")
    spot = jnp.stack([leaf >> 4, (leaf >> 2) & 3, leaf & 3, blk & 1, counts[0], counts[1], ancestry[0], ancestry[1]])

    crossed = shift(basis, xl=1)
    above, below = shift(basis, y=-1), shift(basis, y=1)
    away = couple(1, spot, modes, stiffness)
    came = [shift(piece, c=1) for piece in away]
    kept = couple(0, spot, modes, stiffness)
    both = [add(*pair) for pair in zip(kept, came)]
    crossed, *_ = lax.optimization_barrier((crossed, *both))
    cabove, cbelow = shift(crossed, y=-1), shift(crossed, y=1)
    met2, met13, met0 = (shift(item, xh=1) for item in (both[0], jnp.concatenate(both[1:3]), both[3]))
    met2, above, below = lax.optimization_barrier((met2, above, below))
    own, other = {}, {}
    own[2] = shift(add(both[0][0], met2[0]), z=2)
    mid = TILE // 2
    far1 = shift(jnp.stack([above[:mid], cabove[:mid]]), y=-1)
    far2 = shift(jnp.stack([below[mid:], cbelow[mid:]]), y=1)
    other[2] = shift(own[2][:ROWS], c=1)
    met13, other[2], far1, far2 = lax.optimization_barrier((met13, other[2], far1, far2))
    own[1] = shift(add(both[1][0], met13[0]), z=1)
    own[3] = shift(add(both[2][0], met13[1]), z=3)
    far = jnp.concatenate([far1, far2], axis=1)
    tiles = [basis, above, far[0], below, crossed, cabove, far[1], cbelow]
    part = project([(own[2], other[2])], tiles, whole=True)
    carry1, carry3 = shift(part[0], z=-1), shift(part[1], z=1)
    own[1], own[3], met0, _ = lax.optimization_barrier((own[1], own[3], met0, part[0]))
    own[0] = add(both[3][0], met0[0])
    for d in (1, 3, 0):
        other[d] = shift(own[d][:ROWS], c=1)
    part1, part3 = project([(own[1], other[1]), (own[3], other[3])], tiles, [(0, carry1), (1, carry3)])
    (part0,) = project([(own[0], other[0])], tiles)
    swap = (blk & 1) == 1
    lam = jnp.where(swap, eigen[::-1], eigen)[:, :, None]
    heard = [(shift(part1[h], z=-1), shift(part3[h], z=1)) for h in range(2)]
    sums, scaled = zip(*[scale(lam, [part0[h], *heard[h]]) for h in range(2)])

    coupled = [item for d in range(4) for item in (own[d], other[d])]
    columns = []
    for h in range(2):
        piece = scaled[h]
        if h == 0:
            pieces = [piece] + [shift(piece, z=d) for d in (1, 2, 3)]
            mine = jnp.concatenate(sums, axis=2)
            mine = jnp.where(swap, mine[::-1], mine)
            projection = jnp.pad(mine, ((0, 0), (0, 512 - ROWS), (0, 0)))
            pieces[2], projection = lax.optimization_barrier((pieces[2], projection))
            arrived = pieces[1], pieces[3]
        else:
            piece, *_ = lax.optimization_barrier((piece, *arrived))
            up, down = shift(piece, z=1), shift(piece, z=-1)
            pieces = [piece, up, shift(up[:1], z=1), shift(down[1:], z=-1), down]
            pieces[0], ahead, behind = lax.optimization_barrier((pieces[0], ahead, behind))
        terms = correct(coupled, pieces)
        if h == 1:
            *terms, total = lax.optimization_barrier((*terms, total))
            columns.append(total)
        ahead, behind = shift(terms[2][:1], y=1), shift(terms[2][1:], y=-1)
        ahead = jnp.concatenate([add(terms[1][:1], ahead), terms[1][1:]])
        behind = jnp.concatenate([terms[3][:1], add(terms[3][1:], behind)])
        total = terms[0].astype(F32) + shift(ahead, y=1).astype(F32) + shift(behind, y=-1).astype(F32)
    columns.append(total)
    columns = [total[0] + shift(total[1].astype(BF), xl=1).astype(F32) for total in columns]
    return projection, jnp.concatenate(columns, axis=1)


def solution(mesh):
    placed = (
        P("leaf", "blk", None),
        P("leaf", "blk", None),
        P("leaf", "blk"),
        P("leaf", None),
        P("leaf"),
        P("leaf"),
    )
    return jax.shard_map(
        per_device,
        mesh=mesh,
        in_specs=placed,
        out_specs=(P("leaf", None, "blk"), P("leaf", "blk")),
        check_vma=False,
    )
```

profile of v0, /device:TPU:0, one launch (start us, length us, event | category | flops | bytes accessed | tf_op | source)
XLA Modules:
  0.0 176.7 jit_solution(14949189305200752133)
XLA Ops:
  0.6 0.8 stack.37.spot
  1.4 2.2 %copy-done = bf16[2,512,2048]{2,1,0:T(8,128)(2,1)S(1)} copy-done((bf16[2,512,2048]{2,1,0:T(8,128)(2,1)S(1)}, bf16[2,512,2048]{2,1,0:T(8,128)(2,1)}, u32[]{:S(2)}) %copy-start) | copy-done | bytes 4194328
  3.6 1.2 copy-done.12
  4.8 1.6 couple.3
  7.0 1.6 collective-permute-start.10
  8.6 3.0 %collective-permute-start.6 = (bf16[512,512]{1,0:T(8,128)(2,1)S(1)}, bf16[512,512]{1,0:T(8,128)(2,1)S(1)}, u32[]{:S(2)}, u32[]{:S(2)}) collective-permute-start(bf16[512,512]{1,0:T(8,128)(2,1)S(1)} %copy-done.7), channel_id=1, source_target_pairs={{0,48},{1,49},{2,50},{3,51},{4,52},{5,53},{6,54},{7,55},{8,56},{9,... | collective-permute-start | bytes 1572872 | tf_op jit(solution)/shard_map/ppermute | solution.py:30
  11.6 1.6 couple.2
  14.1 0.9 collective-permute-done.1
  15.1 2.7 %collective-permute-start.5 = (bf16[1,416,512]{2,1,0:T(8,128)(2,1)S(1)}, bf16[1,416,512]{2,1,0:T(8,128)(2,1)S(1)}, u32[]{:S(2)}, u32[]{:S(2)}) collective-permute-start(bf16[1,416,512]{2,1,0:T(8,128)(2,1)S(1)} %add_convert_fusion.4), channel_id=1, source_target_pairs={{0,2},{1,3},{2,0},{3,1},{4,6},{5,7},{6,4},{7,5},{8,10},{9,11},{10,... | collective-permute-start | bytes 1277960 | tf_op jit(solution)/shard_map/ppermute | solution.py:30
  18.0 0.9 collective-permute-start.3
  19.0 2.8 %collective-permute-done.10.refs_6_.refs_8_ = bf16[512,512]{1,0:T(8,128)(2,1)S(1)} collective-permute-done((bf16[512,512]{1,0:T(8,128)(2,1)S(1)}, bf16[512,512]{1,0:T(8,128)(2,1)S(1)}, u32[]{:S(2)}, u32[]{:S(2)}) %collective-permute-start.10) | collective-permute-done | bytes 524320 | tf_op jit(solution)/shard_map/ppermute | solution.py:30
  21.8 1.7 collective-permute-start.13
  23.5 3.0 %collective-permute-start.11 = (bf16[512,512]{1,0:T(8,128)(2,1)S(1)}, bf16[512,512]{1,0:T(8,128)(2,1)S(1)}, u32[]{:S(2)}, u32[]{:S(2)}) collective-permute-start(bf16[512,512]{1,0:T(8,128)(2,1)S(1)} %collective-permute-done.10.refs_6_.refs_8_), channel_id=1, source_target_pairs={{0,48},{1,49},{2,50},{3,51},{4,52},{5,53},{6,54},{7,55},{8,56},{9,... | collective-permute-start | bytes 1572872 | tf_op jit(solution)/shard_map/ppermute | solution.py:30
  26.5 1.2 collective-permute-done.7.refs_5_.refs_7_
  27.7 5.5 %collective-permute-done.5 = bf16[1,416,512]{2,1,0:T(8,128)(2,1)S(1)} collective-permute-done((bf16[1,416,512]{2,1,0:T(8,128)(2,1)S(1)}, bf16[1,416,512]{2,1,0:T(8,128)(2,1)S(1)}, u32[]{:S(2)}, u32[]{:S(2)}) %collective-permute-start.5) | collective-permute-done | bytes 426016 | tf_op jit(solution)/shard_map/ppermute | solution.py:30
  33.3 4.0 %collective-permute-start.8 = (bf16[416,512]{1,0:T(8,128)(2,1)S(1)}, bf16[416,512]{1,0:T(8,128)(2,1)S(1)}, u32[]{:S(2)}, u32[]{:S(2)}) collective-permute-start(bf16[416,512]{1,0:T(8,128)(2,1)S(1)} %fusion.1), channel_id=1, source_target_pairs={{0,8},{1,9},{2,10},{3,11},{4,12},{5,13},{6,14},{7,15},{8,0},{9,1},... | collective-permute-start | bytes 1277960 | tf_op jit(solution)/shard_map/ppermute | solution.py:30
  37.5 1.6 collective-permute-start.14
  39.2 1.8 %collective-permute-start.12 = (bf16[2,256,512]{2,1,0:T(8,128)(2,1)S(1)}, bf16[2,256,512]{2,1,0:T(8,128)(2,1)S(1)}, u32[]{:S(2)}, u32[]{:S(2)}) collective-permute-start(bf16[2,256,512]{2,1,0:T(8,128)(2,1)S(1)} %pad_maximum_fusion.2), channel_id=1, source_target_pairs={{0,48},{1,49},{2,50},{3,51},{4,52},{5,53},{6,54},{7,55},{8,56},{9,... | collective-permute-start | bytes 1572872 | tf_op jit(solution)/shard_map/ppermute | solution.py:30
  41.0 4.7 %collective-permute-done.8.refs_0_.refs_4_ = bf16[416,512]{1,0:T(8,128)(2,1)S(1)} collective-permute-done((bf16[416,512]{1,0:T(8,128)(2,1)S(1)}, bf16[416,512]{1,0:T(8,128)(2,1)S(1)}, u32[]{:S(2)}, u32[]{:S(2)}) %collective-permute-start.8) | collective-permute-done | bytes 426016 | tf_op jit(solution)/shard_map/ppermute | solution.py:30
  45.8 0.9 collective-permute-start.17
  46.7 4.1 %collective-permute-done.3 = bf16[2,416,512]{2,1,0:T(8,128)(2,1)S(1)} collective-permute-done((bf16[2,416,512]{2,1,0:T(8,128)(2,1)S(1)}, bf16[2,416,512]{2,1,0:T(8,128)(2,1)S(1)}, u32[]{:S(2)}, u32[]{:S(2)}) %collective-permute-start.3) | collective-permute-done | bytes 852000 | tf_op jit(solution)/shard_map/ppermute | solution.py:30
  51.5 2.2 %collective-permute-start.15 = (bf16[416,512]{1,0:T(8,128)(2,1)S(1)}, bf16[416,512]{1,0:T(8,128)(2,1)S(1)}, u32[]{:S(2)}, u32[]{:S(2)}) collective-permute-start(bf16[416,512]{1,0:T(8,128)(2,1)S(1)} %get-tuple-element.101), channel_id=1, source_target_pairs={{0,4},{1,5},{2,6},{3,7},{4,8},{5,9},{6,10},{7,11},{8,12},{9,13},{1... | collective-permute-start | bytes 1277960 | tf_op jit(solution)/shard_map/ppermute | solution.py:30
  53.6 2.2 %collective-permute-start.16 = (bf16[416,512]{1,0:T(8,128)(2,1)S(1)}, bf16[416,512]{1,0:T(8,128)(2,1)S(1)}, u32[]{:S(2)}, u32[]{:S(2)}) collective-permute-start(bf16[416,512]{1,0:T(8,128)(2,1)S(1)} %get-tuple-element.100), channel_id=1, source_target_pairs={{0,12},{1,13},{2,14},{3,15},{4,0},{5,1},{6,2},{7,3},{8,4},{9,5},{1... | collective-permute-start | bytes 1277960 | tf_op jit(solution)/shard_map/ppermute | solution.py:30
  56.0 1.1 project.3
  57.1 2.0 %collective-permute-start.21 = (bf16[1,416,512]{2,1,0:T(8,128)(2,1)S(1)}, bf16[1,416,512]{2,1,0:T(8,128)(2,1)S(1)}, u32[]{:S(2)}, u32[]{:S(2)}) collective-permute-start(bf16[1,416,512]{2,1,0:T(8,128)(2,1)S(1)} %get-tuple-element.66), channel_id=1, source_target_pairs={{0,12},{1,13},{2,14},{3,15},{4,0},{5,1},{6,2},{7,3},{8,4},{9,5},{1... | collective-permute-start | bytes 1277960 | tf_op jit(solution)/shard_map/ppermute | solution.py:30
  59.7 6.8 %collective-permute-done.15.refs_0_.refs_2_ = bf16[416,512]{1,0:T(8,128)(2,1)S(1)} collective-permute-done((bf16[416,512]{1,0:T(8,128)(2,1)S(1)}, bf16[416,512]{1,0:T(8,128)(2,1)S(1)}, u32[]{:S(2)}, u32[]{:S(2)}) %collective-permute-start.15) | collective-permute-done | bytes 426016 | tf_op jit(solution)/shard_map/ppermute | solution.py:30
  67.4 0.8 slice_bitcast_fusion.3
  68.2 4.7 %collective-permute-done.21.refs_12_ = bf16[1,416,512]{2,1,0:T(8,128)(2,1)S(1)} collective-permute-done((bf16[1,416,512]{2,1,0:T(8,128)(2,1)S(1)}, bf16[1,416,512]{2,1,0:T(8,128)(2,1)S(1)}, u32[]{:S(2)}, u32[]{:S(2)}) %collective-permute-start.21) | collective-permute-done | bytes 426016 | tf_op jit(solution)/shard_map/ppermute | solution.py:30
  73.4 3.2 %project.5 = (bf16[2,400,256]{2,1,0:T(8,128)(2,1)}, bf16[2,400,256]{2,1,0:T(8,128)(2,1)}, bf16[2,400,256]{2,1,0:T(8,128)(2,1)}, bf16[2,400,256]{2,1,0:T(8,128)(2,1)}) custom-call(bf16[416,512]{1,0:T(8,128)(2,1)S(1)} %collective-permute-done.15.refs_0_.refs_2_, bf16[400,512]{1,0:T(8,128)(2,1)S(1)} %collective-permute-done.19.refs_1_.refs_3_, ...), custom_call_target="tpu_custom_call" | custom-call | flops 1024 | bytes 1024 | tf_op jit(solution)/shard_map/project/pallas_call | solution.py:113
  76.6 3.1 %collective-permute-start.23 = (bf16[2,400,256]{2,1,0:T(8,128)(2,1)}, bf16[2,400,256]{2,1,0:T(8,128)(2,1)}, u32[]{:S(2)}, u32[]{:S(2)}) collective-permute-start(bf16[2,400,256]{2,1,0:T(8,128)(2,1)} %get-tuple-element.72), channel_id=1, source_target_pairs={{0,12},{1,13},{2,14},{3,15},{4,0},{5,1},{6,2},{7,3},{8,4},{9,5},{1... | collective-permute-start | bytes 1228808 | tf_op jit(solution)/shard_map/ppermute | solution.py:30
  79.8 3.2 %collective-permute-start.26 = (bf16[2,400,256]{2,1,0:T(8,128)(2,1)}, bf16[2,400,256]{2,1,0:T(8,128)(2,1)}, u32[]{:S(2)}, u32[]{:S(2)}) collective-permute-start(bf16[2,400,256]{2,1,0:T(8,128)(2,1)} %get-tuple-element.77), channel_id=1, source_target_pairs={{0,12},{1,13},{2,14},{3,15},{4,0},{5,1},{6,2},{7,3},{8,4},{9,5},{1... | collective-permute-start | bytes 1228808 | tf_op jit(solution)/shard_map/ppermute | solution.py:30
  83.1 1.0 copy.8.eigen
  84.1 1.0 copy-done.2
  85.2 1.0 copy-done.4
  86.2 1.0 copy-done.6
  87.3 1.0 copy-done.8
  88.3 1.0 copy-done.10
  89.4 2.1 %project.4 = (bf16[2,400,256]{2,1,0:T(8,128)(2,1)S(1)}, bf16[2,400,256]{2,1,0:T(8,128)(2,1)S(1)}) custom-call(bf16[416,512]{1,0:T(8,128)(2,1)S(1)} %bitcast.37, bf16[400,512]{1,0:T(8,128)(2,1)} %collective-permute-done.18.refs_1_, bf16[512,512]{1,0:T(8,128)(2,1)S(1)} %copy-done.8, bf16[512,512]{1,0:T(8,128)(2,1)S(1)} %collective-permute-done.6.refs_3_.refs_5_, ...), custom_call_target="tpu_custom_call" | custom-call | flops 1024 | bytes 1024 | tf_op jit(solution)/shard_map/project/pallas_call | solution.py:113
  91.5 2.2 %collective-permute-done.24.third = bf16[2,400,256]{2,1,0:T(8,128)(2,1)} collective-permute-done((bf16[2,400,256]{2,1,0:T(8,128)(2,1)}, bf16[2,400,256]{2,1,0:T(8,128)(2,1)}, u32[]{:S(2)}, u32[]{:S(2)}) %collective-permute-start.24) | collective-permute-done | bytes 409632 | tf_op jit(solution)/shard_map/ppermute | solution.py:30
  93.7 1.4 scale.2
  95.2 1.9 %collective-permute-start.28 = (bf16[2,400,256]{2,1,0:T(8,128)(2,1)S(1)}, bf16[2,400,256]{2,1,0:T(8,128)(2,1)S(1)}, u32[]{:S(2)}, u32[]{:S(2)}) collective-permute-start(bf16[2,400,256]{2,1,0:T(8,128)(2,1)S(1)} %get-tuple-element.74.refs_8_), channel_id=1, source_target_pairs={{0,4},{1,5},{2,6},{3,7},{4,8},{5,9},{6,10},{7,11},{8,12},{9,13},{1... | collective-permute-start | bytes 1228808 | tf_op jit(solution)/shard_map/ppermute | solution.py:30
  97.1 1.4 collective-permute-start.29
  98.6 5.5 %collective-permute-done.26.second = bf16[2,400,256]{2,1,0:T(8,128)(2,1)} collective-permute-done((bf16[2,400,256]{2,1,0:T(8,128)(2,1)}, bf16[2,400,256]{2,1,0:T(8,128)(2,1)}, u32[]{:S(2)}, u32[]{:S(2)}) %collective-permute-start.26) | collective-permute-done | bytes 409632 | tf_op jit(solution)/shard_map/ppermute | solution.py:30
  104.1 7.2 %collective-permute-done.27.third = bf16[2,400,256]{2,1,0:T(8,128)(2,1)} collective-permute-done((bf16[2,400,256]{2,1,0:T(8,128)(2,1)}, bf16[2,400,256]{2,1,0:T(8,128)(2,1)}, u32[]{:S(2)}, u32[]{:S(2)}) %collective-permute-start.27) | collective-permute-done | bytes 409632 | tf_op jit(solution)/shard_map/ppermute | solution.py:30
  111.2 1.3 scale.3
  112.8 1.0 pad.4
  113.8 2.3 %collective-permute-done.28.refs_9_ = bf16[2,400,256]{2,1,0:T(8,128)(2,1)S(1)} collective-permute-done((bf16[2,400,256]{2,1,0:T(8,128)(2,1)S(1)}, bf16[2,400,256]{2,1,0:T(8,128)(2,1)S(1)}, u32[]{:S(2)}, u32[]{:S(2)}) %collective-permute-start.28) | collective-permute-done | bytes 409632 | tf_op jit(solution)/shard_map/ppermute | solution.py:30
  116.2 3.3 %correct.2 = (bf16[2,512,256]{2,1,0:T(8,128)(2,1)S(1)}, bf16[2,512,256]{2,1,0:T(8,128)(2,1)S(1)}, bf16[2,512,256]{2,1,0:T(8,128)(2,1)S(1)}, bf16[2,512,256]{2,1,0:T(8,128)(2,1)S(1)}) custom-call(bf16[416,512]{1,0:T(8,128)(2,1)S(1)} %bitcast.38, bf16[400,512]{1,0:T(8,128)(2,1)} %collective-permute-done.18.refs_1_, ...), custom_call_target="tpu_custom_call" | custom-call | flops 1024 | bytes 1024 | tf_op jit(solution)/shard_map/correct/pallas_call | solution.py:162
  119.5 3.1 %collective-permute-start.31 = (bf16[1,512,256]{2,1,0:T(8,128)(2,1)S(1)}, bf16[1,512,256]{2,1,0:T(8,128)(2,1)S(1)}, u32[]{:S(2)}, u32[]{:S(2)}) collective-permute-start(bf16[1,512,256]{2,1,0:T(8,128)(2,1)S(1)} %get-tuple-element.104), channel_id=1, source_target_pairs={{0,48},{1,49},{2,50},{3,51},{4,52},{5,53},{6,54},{7,55},{8,56},{9,... | collective-permute-start | bytes 786440 | tf_op jit(solution)/shard_map/ppermute | solution.py:30
  122.6 3.2 %collective-permute-start.34 = (bf16[2,400,256]{2,1,0:T(8,128)(2,1)S(1)}, bf16[2,400,256]{2,1,0:T(8,128)(2,1)S(1)}, u32[]{:S(2)}, u32[]{:S(2)}) collective-permute-start(bf16[2,400,256]{2,1,0:T(8,128)(2,1)S(1)} %get-tuple-element.87.refs_8_), channel_id=1, source_target_pairs={{0,12},{1,13},{2,14},{3,15},{4,0},{5,1},{6,2},{7,3},{8,4},{9,5},{1... | collective-permute-start | bytes 1228808 | tf_op jit(solution)/shard_map/ppermute | solution.py:30
  125.9 1.3 collective-permute-done.31
  127.3 3.8 %collective-permute-start.37 = (bf16[2,512,256]{2,1,0:T(8,128)(2,1)S(1)}, bf16[2,512,256]{2,1,0:T(8,128)(2,1)S(1)}, u32[]{:S(2)}, u32[]{:S(2)}) collective-permute-start(bf16[2,512,256]{2,1,0:T(8,128)(2,1)S(1)} %pad_maximum_fusion.5), channel_id=1, source_target_pairs={{0,48},{1,49},{2,50},{3,51},{4,52},{5,53},{6,54},{7,55},{8,56},{9,... | collective-permute-start | bytes 1572872 | tf_op jit(solution)/shard_map/ppermute | solution.py:30
  131.1 3.7 %collective-permute-done.30 = bf16[1,512,256]{2,1,0:T(8,128)(2,1)S(1)} collective-permute-done((bf16[1,512,256]{2,1,0:T(8,128)(2,1)S(1)}, bf16[1,512,256]{2,1,0:T(8,128)(2,1)S(1)}, u32[]{:S(2)}, u32[]{:S(2)}) %collective-permute-start.30) | collective-permute-done | bytes 262176 | tf_op jit(solution)/shard_map/ppermute | solution.py:30
  135.1 3.5 %collective-permute-start.35 = (bf16[1,400,256]{2,1,0:T(8,128)(2,1)S(1)}, bf16[1,400,256]{2,1,0:T(8,128)(2,1)S(1)}, u32[]{:S(2)}, u32[]{:S(2)}) collective-permute-start(bf16[1,400,256]{2,1,0:T(8,128)(2,1)S(1)} %slice.139), channel_id=1, source_target_pairs={{0,12},{1,13},{2,14},{3,15},{4,0},{5,1},{6,2},{7,3},{8,4},{9,5},{1... | collective-permute-start | bytes 614408 | tf_op jit(solution)/shard_map/ppermute | solution.py:30
  138.6 3.4 %collective-permute-done.33.refs_10_ = bf16[1,400,256]{2,1,0:T(8,128)(2,1)S(1)} collective-permute-done((bf16[1,400,256]{2,1,0:T(8,128)(2,1)S(1)}, bf16[1,400,256]{2,1,0:T(8,128)(2,1)S(1)}, u32[]{:S(2)}, u32[]{:S(2)}) %collective-permute-start.33) | collective-permute-done | bytes 204832 | tf_op jit(solution)/shard_map/ppermute | solution.py:30
  142.0 3.3 %correct.3 = (bf16[2,512,256]{2,1,0:T(8,128)(2,1)S(1)}, bf16[2,512,256]{2,1,0:T(8,128)(2,1)S(1)}, bf16[2,512,256]{2,1,0:T(8,128)(2,1)S(1)}, bf16[2,512,256]{2,1,0:T(8,128)(2,1)S(1)}) custom-call(bf16[416,512]{1,0:T(8,128)(2,1)S(1)} %bitcast.39, bf16[400,512]{1,0:T(8,128)(2,1)} %collective-permute-done.18.refs_1_, ...), custom_call_target="tpu_custom_call" | custom-call | flops 1024 | bytes 1024 | tf_op jit(solution)/shard_map/correct/pallas_call | solution.py:162
  145.3 2.3 %collective-permute-done.36 = bf16[2,512,256]{2,1,0:T(8,128)(2,1)S(1)} collective-permute-done((bf16[2,512,256]{2,1,0:T(8,128)(2,1)S(1)}, bf16[2,512,256]{2,1,0:T(8,128)(2,1)S(1)}, u32[]{:S(2)}, u32[]{:S(2)}) %collective-permute-start.36) | collective-permute-done | bytes 524320 | tf_op jit(solution)/shard_map/ppermute | solution.py:30
  147.9 3.3 %collective-permute-start.41 = (bf16[1,512,256]{2,1,0:T(8,128)(2,1)S(1)}, bf16[1,512,256]{2,1,0:T(8,128)(2,1)S(1)}, u32[]{:S(2)}, u32[]{:S(2)}) collective-permute-start(bf16[1,512,256]{2,1,0:T(8,128)(2,1)S(1)} %get-tuple-element.103), channel_id=1, source_target_pairs={{0,48},{1,49},{2,50},{3,51},{4,52},{5,53},{6,54},{7,55},{8,56},{9,... | collective-permute-start | bytes 786440 | tf_op jit(solution)/shard_map/ppermute | solution.py:30
  151.3 7.0 %collective-permute-done.39 = bf16[1,512,256]{2,1,0:T(8,128)(2,1)S(1)} collective-permute-done((bf16[1,512,256]{2,1,0:T(8,128)(2,1)S(1)}, bf16[1,512,256]{2,1,0:T(8,128)(2,1)S(1)}, u32[]{:S(2)}, u32[]{:S(2)}) %collective-permute-start.39) | collective-permute-done | bytes 262176 | tf_op jit(solution)/shard_map/ppermute | solution.py:30
  158.6 3.3 %collective-permute-start.42 = (bf16[2,512,256]{2,1,0:T(8,128)(2,1)S(1)}, bf16[2,512,256]{2,1,0:T(8,128)(2,1)S(1)}, u32[]{:S(2)}, u32[]{:S(2)}) collective-permute-start(bf16[2,512,256]{2,1,0:T(8,128)(2,1)S(1)} %pad_maximum_fusion.7), channel_id=1, source_target_pairs={{0,48},{1,49},{2,50},{3,51},{4,52},{5,53},{6,54},{7,55},{8,56},{9,... | collective-permute-start | bytes 1572872 | tf_op jit(solution)/shard_map/ppermute | solution.py:30
  161.9 0.6 collective-permute-start.38
  162.5 6.3 %collective-permute-done.40 = bf16[2,512,256]{2,1,0:T(8,128)(2,1)S(1)} collective-permute-done((bf16[2,512,256]{2,1,0:T(8,128)(2,1)S(1)}, bf16[2,512,256]{2,1,0:T(8,128)(2,1)S(1)}, u32[]{:S(2)}, u32[]{:S(2)}) %collective-permute-start.40) | collective-permute-done | bytes 524320 | tf_op jit(solution)/shard_map/ppermute | solution.py:30
  169.7 5.8 %collective-permute-done.43 = bf16[512,256]{1,0:T(8,128)(2,1)S(1)} collective-permute-done((bf16[512,256]{1,0:T(8,128)(2,1)S(1)}, bf16[512,256]{1,0:T(8,128)(2,1)S(1)}, u32[]{:S(2)}, u32[]{:S(2)}) %collective-permute-start.43) | collective-permute-done | bytes 262176 | tf_op jit(solution)/shard_map/ppermute | solution.py:30
  175.6 1.1 pad_maximum_fusion
  (125 shorter events, 7.7 us)
Async XLA Ops:
  1.4 2.2 %copy-start = (bf16[2,512,2048]{2,1,0:T(8,128)(2,1)S(1)}, bf16[2,512,2048]{2,1,0:T(8,128)(2,1)}, u32[]{:S(2)}) copy-start(bf16[2,512,2048]{2,1,0:T(8,128)(2,1)} %stiffness.3) | copy-start | bytes 12582916
  3.6 1.2 copy-start.12
  4.8 2.2 %copy-start.7 = (bf16[512,512]{1,0:T(8,128)(2,1)S(1)}, bf16[512,512]{1,0:T(8,128)(2,1)}, u32[]{:S(2)}) copy-start(bf16[512,512]{1,0:T(8,128)(2,1)} %refs_4_.1) | copy-start | bytes 1572868
  6.4 6.8 %collective-permute-start.4 = (bf16[1,416,512]{2,1,0:T(8,128)(2,1)S(1)}, bf16[1,416,512]{2,1,0:T(8,128)(2,1)S(1)}, u32[]{:S(2)}, u32[]{:S(2)}) collective-permute-start(bf16[1,416,512]{2,1,0:T(8,128)(2,1)S(1)} %get-tuple-element.57), channel_id=1, source_target_pairs={{0,1},{1,0},{2,3},{3,2},{4,5},{5,4},{6,7},{7,6},{8,9},{9,8},{10,11... | collective-permute-start | bytes 1277960 | tf_op jit(solution)/shard_map/ppermute | solution.py:30
  6.5 6.9 %collective-permute-start.2 = (bf16[1,416,512]{2,1,0:T(8,128)(2,1)S(1)}, bf16[1,416,512]{2,1,0:T(8,128)(2,1)S(1)}, u32[]{:S(2)}, u32[]{:S(2)}) collective-permute-start(bf16[1,416,512]{2,1,0:T(8,128)(2,1)S(1)} %get-tuple-element.55), channel_id=1, source_target_pairs={{0,1},{1,0},{2,3},{3,2},{4,5},{5,4},{6,7},{7,6},{8,9},{9,8},{10,11... | collective-permute-start | bytes 1277960 | tf_op jit(solution)/shard_map/ppermute | solution.py:30
  7.0 14.8 %collective-permute-start.10 = (bf16[512,512]{1,0:T(8,128)(2,1)S(1)}, bf16[512,512]{1,0:T(8,128)(2,1)S(1)}, u32[]{:S(2)}, u32[]{:S(2)}) collective-permute-start(bf16[512,512]{1,0:T(8,128)(2,1)S(1)} %copy-done.7), channel_id=1, source_target_pairs={{0,64},{1,65},{2,66},{3,67},{4,68},{5,69},{6,70},{7,71},{8,72},{9,... | collective-permute-start | bytes 1572872 | tf_op jit(solution)/shard_map/ppermute | solution.py:30
  8.6 14.9 %collective-permute-start.6 = (bf16[512,512]{1,0:T(8,128)(2,1)S(1)}, bf16[512,512]{1,0:T(8,128)(2,1)S(1)}, u32[]{:S(2)}, u32[]{:S(2)}) collective-permute-start(bf16[512,512]{1,0:T(8,128)(2,1)S(1)} %copy-done.7), channel_id=1, source_target_pairs={{0,48},{1,49},{2,50},{3,51},{4,52},{5,53},{6,54},{7,55},{8,56},{9,... | collective-permute-start | bytes 1572872 | tf_op jit(solution)/shard_map/ppermute | solution.py:30
  11.6 16.1 %collective-permute-start.7 = (bf16[512,512]{1,0:T(8,128)(2,1)S(1)}, bf16[512,512]{1,0:T(8,128)(2,1)S(1)}, u32[]{:S(2)}, u32[]{:S(2)}) collective-permute-start(bf16[512,512]{1,0:T(8,128)(2,1)S(1)} %copy-done.7), channel_id=1, source_target_pairs={{0,16},{1,17},{2,18},{3,19},{4,20},{5,21},{6,22},{7,23},{8,24},{9,... | collective-permute-start | bytes 1572872 | tf_op jit(solution)/shard_map/ppermute | solution.py:30
  13.2 1.8 %collective-permute-start.1 = (bf16[1,416,512]{2,1,0:T(8,128)(2,1)S(1)}, bf16[1,416,512]{2,1,0:T(8,128)(2,1)S(1)}, u32[]{:S(2)}, u32[]{:S(2)}) collective-permute-start(bf16[1,416,512]{2,1,0:T(8,128)(2,1)S(1)} %get-tuple-element.53), channel_id=1, source_target_pairs={{0,1},{1,0},{2,3},{3,2},{4,5},{5,4},{6,7},{7,6},{8,9},{9,8},{10,11... | collective-permute-start | bytes 1277960 | tf_op jit(solution)/shard_map/ppermute | solution.py:30
  13.5 4.6 %collective-permute-start = (bf16[1,416,512]{2,1,0:T(8,128)(2,1)S(1)}, bf16[1,416,512]{2,1,0:T(8,128)(2,1)S(1)}, u32[]{:S(2)}, u32[]{:S(2)}) collective-permute-start(bf16[1,416,512]{2,1,0:T(8,128)(2,1)S(1)} %get-tuple-element.51), channel_id=1, source_target_pairs={{0,1},{1,0},{2,3},{3,2},{4,5},{5,4},{6,7},{7,6},{8,9},{9,8},{10,11... | collective-permute-start | bytes 1277960 | tf_op jit(solution)/shard_map/ppermute | solution.py:30
  15.1 18.1 %collective-permute-start.5 = (bf16[1,416,512]{2,1,0:T(8,128)(2,1)S(1)}, bf16[1,416,512]{2,1,0:T(8,128)(2,1)S(1)}, u32[]{:S(2)}, u32[]{:S(2)}) collective-permute-start(bf16[1,416,512]{2,1,0:T(8,128)(2,1)S(1)} %add_convert_fusion.4), channel_id=1, source_target_pairs={{0,2},{1,3},{2,0},{3,1},{4,6},{5,7},{6,4},{7,5},{8,10},{9,11},{10,... | collective-permute-start | bytes 1277960 | tf_op jit(solution)/shard_map/ppermute | solution.py:30
  18.0 32.7 %collective-permute-start.3 = (bf16[2,416,512]{2,1,0:T(8,128)(2,1)S(1)}, bf16[2,416,512]{2,1,0:T(8,128)(2,1)S(1)}, u32[]{:S(2)}, u32[]{:S(2)}) collective-permute-start(bf16[2,416,512]{2,1,0:T(8,128)(2,1)S(1)} %pad_maximum_fusion.1), channel_id=1, source_target_pairs={{0,2},{1,3},{2,0},{3,1},{4,6},{5,7},{6,4},{7,5},{8,10},{9,11},{10,... | collective-permute-start | bytes 2555912 | tf_op jit(solution)/shard_map/ppermute | solution.py:30
  21.8 51.6 %copy-start.9 = (bf16[512,512]{1,0:T(8,128)(2,1)}, bf16[512,512]{1,0:T(8,128)(2,1)S(1)}, u32[]{:S(2)}) copy-start(bf16[512,512]{1,0:T(8,128)(2,1)S(1)} %collective-permute-done.10.refs_6_.refs_8_) | copy-start | bytes 1572868
  21.8 15.6 %collective-permute-start.13 = (bf16[512,512]{1,0:T(8,128)(2,1)S(1)}, bf16[512,512]{1,0:T(8,128)(2,1)S(1)}, u32[]{:S(2)}, u32[]{:S(2)}) collective-permute-start(bf16[512,512]{1,0:T(8,128)(2,1)S(1)} %collective-permute-done.10.refs_6_.refs_8_), channel_id=1, source_target_pairs={{0,16},{1,17},{2,18},{3,19},{4,20},{5,21},{6,22},{7,23},{8,24},{9,... | collective-permute-start | bytes 1572872 | tf_op jit(solution)/shard_map/ppermute | solution.py:30
  23.5 15.6 %collective-permute-start.11 = (bf16[512,512]{1,0:T(8,128)(2,1)S(1)}, bf16[512,512]{1,0:T(8,128)(2,1)S(1)}, u32[]{:S(2)}, u32[]{:S(2)}) collective-permute-start(bf16[512,512]{1,0:T(8,128)(2,1)S(1)} %collective-permute-done.10.refs_6_.refs_8_), channel_id=1, source_target_pairs={{0,48},{1,49},{2,50},{3,51},{4,52},{5,53},{6,54},{7,55},{8,56},{9,... | collective-permute-start | bytes 1572872 | tf_op jit(solution)/shard_map/ppermute | solution.py:30
  27.7 45.7 %copy-start.1 = (bf16[512,512]{1,0:T(8,128)(2,1)}, bf16[512,512]{1,0:T(8,128)(2,1)S(1)}, u32[]{:S(2)}) copy-start(bf16[512,512]{1,0:T(8,128)(2,1)S(1)} %collective-permute-done.7.refs_5_.refs_7_) | copy-start | bytes 1572868
  33.3 12.4 %collective-permute-start.8 = (bf16[416,512]{1,0:T(8,128)(2,1)S(1)}, bf16[416,512]{1,0:T(8,128)(2,1)S(1)}, u32[]{:S(2)}, u32[]{:S(2)}) collective-permute-start(bf16[416,512]{1,0:T(8,128)(2,1)S(1)} %fusion.1), channel_id=1, source_target_pairs={{0,8},{1,9},{2,10},{3,11},{4,12},{5,13},{6,14},{7,15},{8,0},{9,1},... | collective-permute-start | bytes 1277960 | tf_op jit(solution)/shard_map/ppermute | solution.py:30
  37.4 36.0 %copy-start.3 = (bf16[512,512]{1,0:T(8,128)(2,1)}, bf16[512,512]{1,0:T(8,128)(2,1)S(1)}, u32[]{:S(2)}) copy-start(bf16[512,512]{1,0:T(8,128)(2,1)S(1)} %collective-permute-done.13.refs_9_.refs_11_) | copy-start | bytes 1572868
  37.5 13.7 %collective-permute-start.14 = (bf16[2,256,512]{2,1,0:T(8,128)(2,1)S(1)}, bf16[2,256,512]{2,1,0:T(8,128)(2,1)S(1)}, u32[]{:S(2)}, u32[]{:S(2)}) collective-permute-start(bf16[2,256,512]{2,1,0:T(8,128)(2,1)S(1)} %pad_maximum_fusion.3), channel_id=1, source_target_pairs={{0,16},{1,17},{2,18},{3,19},{4,20},{5,21},{6,22},{7,23},{8,24},{9,... | collective-permute-start | bytes 1572872 | tf_op jit(solution)/shard_map/ppermute | solution.py:30
  39.1 34.3 %copy-start.5 = (bf16[512,512]{1,0:T(8,128)(2,1)}, bf16[512,512]{1,0:T(8,128)(2,1)S(1)}, u32[]{:S(2)}) copy-start(bf16[512,512]{1,0:T(8,128)(2,1)S(1)} %collective-permute-done.11.refs_7_.refs_9_) | copy-start | bytes 1572868
  39.2 12.1 %collective-permute-start.12 = (bf16[2,256,512]{2,1,0:T(8,128)(2,1)S(1)}, bf16[2,256,512]{2,1,0:T(8,128)(2,1)S(1)}, u32[]{:S(2)}, u32[]{:S(2)}) collective-permute-start(bf16[2,256,512]{2,1,0:T(8,128)(2,1)S(1)} %pad_maximum_fusion.2), channel_id=1, source_target_pairs={{0,48},{1,49},{2,50},{3,51},{4,52},{5,53},{6,54},{7,55},{8,56},{9,... | collective-permute-start | bytes 1572872 | tf_op jit(solution)/shard_map/ppermute | solution.py:30
  45.7 5.5 %collective-permute-start.9 = (bf16[400,512]{1,0:T(8,128)(2,1)S(1)}, bf16[400,512]{1,0:T(8,128)(2,1)S(1)}, u32[]{:S(2)}, u32[]{:S(2)}) collective-permute-start(bf16[400,512]{1,0:T(8,128)(2,1)S(1)} %slice.132), channel_id=1, source_target_pairs={{0,1},{1,0},{2,3},{3,2},{4,5},{5,4},{6,7},{7,6},{8,9},{9,8},{10,11... | collective-permute-start | bytes 1228808 | tf_op jit(solution)/shard_map/ppermute | solution.py:30
  45.8 13.9 %collective-permute-start.17 = (bf16[1,416,512]{2,1,0:T(8,128)(2,1)S(1)}, bf16[1,416,512]{2,1,0:T(8,128)(2,1)S(1)}, u32[]{:S(2)}, u32[]{:S(2)}) collective-permute-start(bf16[1,416,512]{2,1,0:T(8,128)(2,1)S(1)} %add_convert_fusion.7), channel_id=1, source_target_pairs={{0,2},{1,3},{2,0},{3,1},{4,6},{5,7},{6,4},{7,5},{8,10},{9,11},{10,... | collective-permute-start | bytes 1277960 | tf_op jit(solution)/shard_map/ppermute | solution.py:30
  51.2 5.8 %copy-start.13 = (bf16[400,512]{1,0:T(8,128)(2,1)}, bf16[400,512]{1,0:T(8,128)(2,1)S(1)}, u32[]{:S(2)}) copy-start(bf16[400,512]{1,0:T(8,128)(2,1)S(1)} %collective-permute-done.9.refs_1_.refs_5_) | copy-start | bytes 1228804
  51.5 15.0 %collective-permute-start.15 = (bf16[416,512]{1,0:T(8,128)(2,1)S(1)}, bf16[416,512]{1,0:T(8,128)(2,1)S(1)}, u32[]{:S(2)}, u32[]{:S(2)}) collective-permute-start(bf16[416,512]{1,0:T(8,128)(2,1)S(1)} %get-tuple-element.101), channel_id=1, source_target_pairs={{0,4},{1,5},{2,6},{3,7},{4,8},{5,9},{6,10},{7,11},{8,12},{9,13},{1... | collective-permute-start | bytes 1277960 | tf_op jit(solution)/shard_map/ppermute | solution.py:30
  53.6 12.9 %collective-permute-start.16 = (bf16[416,512]{1,0:T(8,128)(2,1)S(1)}, bf16[416,512]{1,0:T(8,128)(2,1)S(1)}, u32[]{:S(2)}, u32[]{:S(2)}) collective-permute-start(bf16[416,512]{1,0:T(8,128)(2,1)S(1)} %get-tuple-element.100), channel_id=1, source_target_pairs={{0,12},{1,13},{2,14},{3,15},{4,0},{5,1},{6,2},{7,3},{8,4},{9,5},{1... | collective-permute-start | bytes 1277960 | tf_op jit(solution)/shard_map/ppermute | solution.py:30
  57.1 15.8 %collective-permute-start.21 = (bf16[1,416,512]{2,1,0:T(8,128)(2,1)S(1)}, bf16[1,416,512]{2,1,0:T(8,128)(2,1)S(1)}, u32[]{:S(2)}, u32[]{:S(2)}) collective-permute-start(bf16[1,416,512]{2,1,0:T(8,128)(2,1)S(1)} %get-tuple-element.66), channel_id=1, source_target_pairs={{0,12},{1,13},{2,14},{3,15},{4,0},{5,1},{6,2},{7,3},{8,4},{9,5},{1... | collective-permute-start | bytes 1277960 | tf_op jit(solution)/shard_map/ppermute | solution.py:30
  59.1 14.3 %collective-permute-start.22 = (bf16[1,416,512]{2,1,0:T(8,128)(2,1)S(1)}, bf16[1,416,512]{2,1,0:T(8,128)(2,1)S(1)}, u32[]{:S(2)}, u32[]{:S(2)}) collective-permute-start(bf16[1,416,512]{2,1,0:T(8,128)(2,1)S(1)} %get-tuple-element.71), channel_id=1, source_target_pairs={{0,4},{1,5},{2,6},{3,7},{4,8},{5,9},{6,10},{7,11},{8,12},{9,13},{1... | collective-permute-start | bytes 1277960 | tf_op jit(solution)/shard_map/ppermute | solution.py:30
  66.5 6.8 %collective-permute-start.19 = (bf16[400,512]{1,0:T(8,128)(2,1)S(1)}, bf16[400,512]{1,0:T(8,128)(2,1)S(1)}, u32[]{:S(2)}, u32[]{:S(2)}) collective-permute-start(bf16[400,512]{1,0:T(8,128)(2,1)S(1)} %slice.112), channel_id=1, source_target_pairs={{0,1},{1,0},{2,3},{3,2},{4,5},{5,4},{6,7},{7,6},{8,9},{9,8},{10,11... | collective-permute-start | bytes 1228808 | tf_op jit(solution)/shard_map/ppermute | solution.py:30
  66.7 16.3 %copy-start.19 = (f32[2,512]{1,0:T(2,128)S(1)}, f32[2,512]{1,0:T(2,128)}, u32[]{:S(2)}) copy-start(f32[2,512]{1,0:T(2,128)} %param.9) | copy-start | bytes 12292
  66.7 6.7 %collective-permute-start.20 = (bf16[400,512]{1,0:T(8,128)(2,1)S(1)}, bf16[400,512]{1,0:T(8,128)(2,1)S(1)}, u32[]{:S(2)}, u32[]{:S(2)}) collective-permute-start(bf16[400,512]{1,0:T(8,128)(2,1)S(1)} %slice.113), channel_id=1, source_target_pairs={{0,1},{1,0},{2,3},{3,2},{4,5},{5,4},{6,7},{7,6},{8,9},{9,8},{10,11... | collective-permute-start | bytes 1228808 | tf_op jit(solution)/shard_map/ppermute | solution.py:30
  68.1 16.0 %collective-permute-start.18 = (bf16[400,512]{1,0:T(8,128)(2,1)}, bf16[400,512]{1,0:T(8,128)(2,1)}, u32[]{:S(2)}, u32[]{:S(2)}) collective-permute-start(bf16[400,512]{1,0:T(8,128)(2,1)} %slice_bitcast_fusion.3), channel_id=1, source_target_pairs={{0,1},{1,0},{2,3},{3,2},{4,5},{5,4},{6,7},{7,6},{8,9},{9,8},{10,11... | collective-permute-start | bytes 1228808 | tf_op jit(solution)/shard_map/ppermute | solution.py:30
  73.4 3.3 %copy-start.15 = (bf16[400,512]{1,0:T(8,128)(2,1)}, bf16[400,512]{1,0:T(8,128)(2,1)S(1)}, u32[]{:S(2)}) copy-start(bf16[400,512]{1,0:T(8,128)(2,1)S(1)} %collective-permute-done.19.refs_1_.refs_3_) | copy-start | bytes 1228804
  73.4 3.2 %copy-start.17 = (bf16[400,512]{1,0:T(8,128)(2,1)}, bf16[400,512]{1,0:T(8,128)(2,1)S(1)}, u32[]{:S(2)}) copy-start(bf16[400,512]{1,0:T(8,128)(2,1)S(1)} %collective-permute-done.20.refs_3_.refs_7_) | copy-start | bytes 1228804
  76.6 14.8 %collective-permute-start.23 = (bf16[2,400,256]{2,1,0:T(8,128)(2,1)}, bf16[2,400,256]{2,1,0:T(8,128)(2,1)}, u32[]{:S(2)}, u32[]{:S(2)}) collective-permute-start(bf16[2,400,256]{2,1,0:T(8,128)(2,1)} %get-tuple-element.72), channel_id=1, source_target_pairs={{0,12},{1,13},{2,14},{3,15},{4,0},{5,1},{6,2},{7,3},{8,4},{9,5},{1... | collective-permute-start | bytes 1228808 | tf_op jit(solution)/shard_map/ppermute | solution.py:30
  79.7 13.9 %collective-permute-start.24 = (bf16[2,400,256]{2,1,0:T(8,128)(2,1)}, bf16[2,400,256]{2,1,0:T(8,128)(2,1)}, u32[]{:S(2)}, u32[]{:S(2)}) collective-permute-start(bf16[2,400,256]{2,1,0:T(8,128)(2,1)} %get-tuple-element.73), channel_id=1, source_target_pairs={{0,4},{1,5},{2,6},{3,7},{4,8},{5,9},{6,10},{7,11},{8,12},{9,13},{1... | collective-permute-start | bytes 1228808 | tf_op jit(solution)/shard_map/ppermute | solution.py:30
  79.8 24.3 %collective-permute-start.26 = (bf16[2,400,256]{2,1,0:T(8,128)(2,1)}, bf16[2,400,256]{2,1,0:T(8,128)(2,1)}, u32[]{:S(2)}, u32[]{:S(2)}) collective-permute-start(bf16[2,400,256]{2,1,0:T(8,128)(2,1)} %get-tuple-element.77), channel_id=1, source_target_pairs={{0,12},{1,13},{2,14},{3,15},{4,0},{5,1},{6,2},{7,3},{8,4},{9,5},{1... | collective-permute-start | bytes 1228808 | tf_op jit(solution)/shard_map/ppermute | solution.py:30
  83.0 28.2 %collective-permute-start.27 = (bf16[2,400,256]{2,1,0:T(8,128)(2,1)}, bf16[2,400,256]{2,1,0:T(8,128)(2,1)}, u32[]{:S(2)}, u32[]{:S(2)}) collective-permute-start(bf16[2,400,256]{2,1,0:T(8,128)(2,1)} %get-tuple-element.78), channel_id=1, source_target_pairs={{0,4},{1,5},{2,6},{3,7},{4,8},{5,9},{6,10},{7,11},{8,12},{9,13},{1... | collective-permute-start | bytes 1228808 | tf_op jit(solution)/shard_map/ppermute | solution.py:30
  84.1 1.0 copy-start.2
  85.2 1.0 copy-start.4
  86.2 1.0 copy-start.6
  87.3 1.0 copy-start.8
  88.3 1.0 copy-start.10
  89.4 4.3 %copy-start.11 = (f32[2,512,1]{2,1,0:T(8,128)S(1)}, f32[2,512,1]{2,1,0:T(8,128)}, u32[]{:S(2)}) copy-start(f32[2,512,1]{2,1,0:T(8,128)} %copy.8.eigen) | copy-start | bytes 12292
  93.7 22.5 %copy-start.14 = (bf16[400,512]{1,0:T(8,128)(2,1)S(1)}, bf16[400,512]{1,0:T(8,128)(2,1)}, u32[]{:S(2)}) copy-start(bf16[400,512]{1,0:T(8,128)(2,1)} %copy-done.13) | copy-start | bytes 1228804
  93.7 22.5 %copy-start.16 = (bf16[400,512]{1,0:T(8,128)(2,1)S(1)}, bf16[400,512]{1,0:T(8,128)(2,1)}, u32[]{:S(2)}) copy-start(bf16[400,512]{1,0:T(8,128)(2,1)} %copy-done.15) | copy-start | bytes 1228804
  93.7 22.5 %copy-start.18 = (bf16[400,512]{1,0:T(8,128)(2,1)S(1)}, bf16[400,512]{1,0:T(8,128)(2,1)}, u32[]{:S(2)}) copy-start(bf16[400,512]{1,0:T(8,128)(2,1)} %copy-done.17) | copy-start | bytes 1228804
  95.1 18.7 %collective-permute-start.25 = (bf16[2,400,256]{2,1,0:T(8,128)(2,1)S(1)}, bf16[2,400,256]{2,1,0:T(8,128)(2,1)S(1)}, u32[]{:S(2)}, u32[]{:S(2)}) collective-permute-start(bf16[2,400,256]{2,1,0:T(8,128)(2,1)S(1)} %get-tuple-element.74.refs_8_), channel_id=1, source_target_pairs={{0,8},{1,9},{2,10},{3,11},{4,12},{5,13},{6,14},{7,15},{8,0},{9,1},... | collective-permute-start | bytes 1228808 | tf_op jit(solution)/shard_map/ppermute | solution.py:30
  95.2 20.9 %collective-permute-start.28 = (bf16[2,400,256]{2,1,0:T(8,128)(2,1)S(1)}, bf16[2,400,256]{2,1,0:T(8,128)(2,1)S(1)}, u32[]{:S(2)}, u32[]{:S(2)}) collective-permute-start(bf16[2,400,256]{2,1,0:T(8,128)(2,1)S(1)} %get-tuple-element.74.refs_8_), channel_id=1, source_target_pairs={{0,4},{1,5},{2,6},{3,7},{4,8},{5,9},{6,10},{7,11},{8,12},{9,13},{1... | collective-permute-start | bytes 1228808 | tf_op jit(solution)/shard_map/ppermute | solution.py:30
  97.1 19.0 %collective-permute-start.29 = (bf16[2,400,256]{2,1,0:T(8,128)(2,1)S(1)}, bf16[2,400,256]{2,1,0:T(8,128)(2,1)S(1)}, u32[]{:S(2)}, u32[]{:S(2)}) collective-permute-start(bf16[2,400,256]{2,1,0:T(8,128)(2,1)S(1)} %get-tuple-element.74.refs_8_), channel_id=1, source_target_pairs={{0,12},{1,13},{2,14},{3,15},{4,0},{5,1},{6,2},{7,3},{8,4},{9,5},{1... | collective-permute-start | bytes 1228808 | tf_op jit(solution)/shard_map/ppermute | solution.py:30
  119.5 7.7 %collective-permute-start.31 = (bf16[1,512,256]{2,1,0:T(8,128)(2,1)S(1)}, bf16[1,512,256]{2,1,0:T(8,128)(2,1)S(1)}, u32[]{:S(2)}, u32[]{:S(2)}) collective-permute-start(bf16[1,512,256]{2,1,0:T(8,128)(2,1)S(1)} %get-tuple-element.104), channel_id=1, source_target_pairs={{0,48},{1,49},{2,50},{3,51},{4,52},{5,53},{6,54},{7,55},{8,56},{9,... | collective-permute-start | bytes 786440 | tf_op jit(solution)/shard_map/ppermute | solution.py:30
  122.6 12.4 %collective-permute-start.32 = (bf16[2,400,256]{2,1,0:T(8,128)(2,1)S(1)}, bf16[2,400,256]{2,1,0:T(8,128)(2,1)S(1)}, u32[]{:S(2)}, u32[]{:S(2)}) collective-permute-start(bf16[2,400,256]{2,1,0:T(8,128)(2,1)S(1)} %get-tuple-element.87.refs_8_), channel_id=1, source_target_pairs={{0,4},{1,5},{2,6},{3,7},{4,8},{5,9},{6,10},{7,11},{8,12},{9,13},{1... | collective-permute-start | bytes 1228808 | tf_op jit(solution)/shard_map/ppermute | solution.py:30
  122.6 12.5 %collective-permute-start.34 = (bf16[2,400,256]{2,1,0:T(8,128)(2,1)S(1)}, bf16[2,400,256]{2,1,0:T(8,128)(2,1)S(1)}, u32[]{:S(2)}, u32[]{:S(2)}) collective-permute-start(bf16[2,400,256]{2,1,0:T(8,128)(2,1)S(1)} %get-tuple-element.87.refs_8_), channel_id=1, source_target_pairs={{0,12},{1,13},{2,14},{3,15},{4,0},{5,1},{6,2},{7,3},{8,4},{9,5},{1... | collective-permute-start | bytes 1228808 | tf_op jit(solution)/shard_map/ppermute | solution.py:30
  125.8 8.9 %collective-permute-start.30 = (bf16[1,512,256]{2,1,0:T(8,128)(2,1)S(1)}, bf16[1,512,256]{2,1,0:T(8,128)(2,1)S(1)}, u32[]{:S(2)}, u32[]{:S(2)}) collective-permute-start(bf16[1,512,256]{2,1,0:T(8,128)(2,1)S(1)} %get-tuple-element.105), channel_id=1, source_target_pairs={{0,16},{1,17},{2,18},{3,19},{4,20},{5,21},{6,22},{7,23},{8,24},{9,... | collective-permute-start | bytes 786440 | tf_op jit(solution)/shard_map/ppermute | solution.py:30
  127.3 18.0 %collective-permute-start.37 = (bf16[2,512,256]{2,1,0:T(8,128)(2,1)S(1)}, bf16[2,512,256]{2,1,0:T(8,128)(2,1)S(1)}, u32[]{:S(2)}, u32[]{:S(2)}) collective-permute-start(bf16[2,512,256]{2,1,0:T(8,128)(2,1)S(1)} %pad_maximum_fusion.5), channel_id=1, source_target_pairs={{0,48},{1,49},{2,50},{3,51},{4,52},{5,53},{6,54},{7,55},{8,56},{9,... | collective-permute-start | bytes 1572872 | tf_op jit(solution)/shard_map/ppermute | solution.py:30
  134.9 12.7 %collective-permute-start.36 = (bf16[2,512,256]{2,1,0:T(8,128)(2,1)S(1)}, bf16[2,512,256]{2,1,0:T(8,128)(2,1)S(1)}, u32[]{:S(2)}, u32[]{:S(2)}) collective-permute-start(bf16[2,512,256]{2,1,0:T(8,128)(2,1)S(1)} %pad_maximum_fusion.4), channel_id=1, source_target_pairs={{0,16},{1,17},{2,18},{3,19},{4,20},{5,21},{6,22},{7,23},{8,24},{9,... | collective-permute-start | bytes 1572872 | tf_op jit(solution)/shard_map/ppermute | solution.py:30
  135.0 7.0 %collective-permute-start.33 = (bf16[1,400,256]{2,1,0:T(8,128)(2,1)S(1)}, bf16[1,400,256]{2,1,0:T(8,128)(2,1)S(1)}, u32[]{:S(2)}, u32[]{:S(2)}) collective-permute-start(bf16[1,400,256]{2,1,0:T(8,128)(2,1)S(1)} %slice.138), channel_id=1, source_target_pairs={{0,4},{1,5},{2,6},{3,7},{4,8},{5,9},{6,10},{7,11},{8,12},{9,13},{1... | collective-permute-start | bytes 614408 | tf_op jit(solution)/shard_map/ppermute | solution.py:30
  135.1 6.9 %collective-permute-start.35 = (bf16[1,400,256]{2,1,0:T(8,128)(2,1)S(1)}, bf16[1,400,256]{2,1,0:T(8,128)(2,1)S(1)}, u32[]{:S(2)}, u32[]{:S(2)}) collective-permute-start(bf16[1,400,256]{2,1,0:T(8,128)(2,1)S(1)} %slice.139), channel_id=1, source_target_pairs={{0,12},{1,13},{2,14},{3,15},{4,0},{5,1},{6,2},{7,3},{8,4},{9,5},{1... | collective-permute-start | bytes 614408 | tf_op jit(solution)/shard_map/ppermute | solution.py:30
  147.8 10.4 %collective-permute-start.39 = (bf16[1,512,256]{2,1,0:T(8,128)(2,1)S(1)}, bf16[1,512,256]{2,1,0:T(8,128)(2,1)S(1)}, u32[]{:S(2)}, u32[]{:S(2)}) collective-permute-start(bf16[1,512,256]{2,1,0:T(8,128)(2,1)S(1)} %get-tuple-element.102), channel_id=1, source_target_pairs={{0,16},{1,17},{2,18},{3,19},{4,20},{5,21},{6,22},{7,23},{8,24},{9,... | collective-permute-start | bytes 786440 | tf_op jit(solution)/shard_map/ppermute | solution.py:30
  147.9 10.5 %collective-permute-start.41 = (bf16[1,512,256]{2,1,0:T(8,128)(2,1)S(1)}, bf16[1,512,256]{2,1,0:T(8,128)(2,1)S(1)}, u32[]{:S(2)}, u32[]{:S(2)}) collective-permute-start(bf16[1,512,256]{2,1,0:T(8,128)(2,1)S(1)} %get-tuple-element.103), channel_id=1, source_target_pairs={{0,48},{1,49},{2,50},{3,51},{4,52},{5,53},{6,54},{7,55},{8,56},{9,... | collective-permute-start | bytes 786440 | tf_op jit(solution)/shard_map/ppermute | solution.py:30
  158.4 10.5 %collective-permute-start.40 = (bf16[2,512,256]{2,1,0:T(8,128)(2,1)S(1)}, bf16[2,512,256]{2,1,0:T(8,128)(2,1)S(1)}, u32[]{:S(2)}, u32[]{:S(2)}) collective-permute-start(bf16[2,512,256]{2,1,0:T(8,128)(2,1)S(1)} %pad_maximum_fusion.6), channel_id=1, source_target_pairs={{0,16},{1,17},{2,18},{3,19},{4,20},{5,21},{6,22},{7,23},{8,24},{9,... | collective-permute-start | bytes 1572872 | tf_op jit(solution)/shard_map/ppermute | solution.py:30
  158.6 10.2 %collective-permute-start.42 = (bf16[2,512,256]{2,1,0:T(8,128)(2,1)S(1)}, bf16[2,512,256]{2,1,0:T(8,128)(2,1)S(1)}, u32[]{:S(2)}, u32[]{:S(2)}) collective-permute-start(bf16[2,512,256]{2,1,0:T(8,128)(2,1)S(1)} %pad_maximum_fusion.7), channel_id=1, source_target_pairs={{0,48},{1,49},{2,50},{3,51},{4,52},{5,53},{6,54},{7,55},{8,56},{9,... | collective-permute-start | bytes 1572872 | tf_op jit(solution)/shard_map/ppermute | solution.py:30
  161.9 7.8 %collective-permute-start.38 = (bf16[512,256]{1,0:T(8,128)(2,1)S(1)}, bf16[512,256]{1,0:T(8,128)(2,1)S(1)}, u32[]{:S(2)}, u32[]{:S(2)}) collective-permute-start(bf16[512,256]{1,0:T(8,128)(2,1)S(1)} %fusion.4), channel_id=1, source_target_pairs={{0,64},{1,65},{2,66},{3,67},{4,68},{5,69},{6,70},{7,71},{8,72},{9,... | collective-permute-start | bytes 786440 | tf_op jit(solution)/shard_map/ppermute | solution.py:30
  169.1 6.5 %collective-permute-start.43 = (bf16[512,256]{1,0:T(8,128)(2,1)S(1)}, bf16[512,256]{1,0:T(8,128)(2,1)S(1)}, u32[]{:S(2)}, u32[]{:S(2)}) collective-permute-start(bf16[512,256]{1,0:T(8,128)(2,1)S(1)} %fusion.5), channel_id=1, source_target_pairs={{0,64},{1,65},{2,66},{3,67},{4,68},{5,69},{6,70},{7,71},{8,72},{9,... | collective-permute-start | bytes 786440 | tf_op jit(solution)/shard_map/ppermute | solution.py:30
where the time goes:
time: 178 us; the launch traced here: 177 us
  waiting for transfers between devices  79.3 us (45%)
  starting transfers between devices  61 us (34%)
  Pallas kernels  18.9 us (11%)
  local copies, waits for them, and re-layouts  13 us (7%)
  other arithmetic  3.25 us (2%)
    ppermute x44, waiting for transfers between devices, shift(): return lax.ppermute(value, AXES, pairs)  79.3 us
    ppermute x44, starting transfers between devices, shift(): return lax.ppermute(value, AXES, pairs)  61 us
    unnamed x42, local copies, waits for them, and re-layouts  8.73 us
    pallas_call x2, Pallas kernels, correct(): pl.pallas_call(kernel, out_shape=[jax.ShapeDtypeStruct((2, TILE, width),...  6.52 us
    pallas_call x3, Pallas kernels, project(): pl.pallas_call(kernel, out_shape=[jax.ShapeDtypeStruct(shape, BF) for sha...  6.35 us
  transfers between devices with their start and end apart: 44, of which 23 were waited for; matrix products, arithmetic and copies ran while one was open for 3% of the time, Pallas kernels for 8%

commit v1 on v0

--- a/solution.py
+++ b/solution.py
@@ -122,7 +122,7 @@
     )(*[item for pair in sides for item in pair], *tiles, *[item for _, item in carry])
     if whole:
         return flat
-    return [flat[n * len(WIDTHS) : (n + 1) * len(WIDTHS)] for n in range(count)]
+    return [list(flat[n * len(WIDTHS) : (n + 1) * len(WIDTHS)]) for n in range(count)]
 
 
 def scale(eigen, parts):
@@ -143,32 +143,55 @@
     )(eigen, *parts)
 
 
-def correct(coupled, scaled):
-    width = scaled[0].shape[2]
+def places_in(coupled):
+    tags = sum(tag_of(own) * (0.5 * 64**d) for d, own in enumerate(coupled[::2]))
+    places = jnp.max(tags).astype(jnp.int32)
+    return [(places >> (3 * n)) & 7 for n in range(len(coupled))]
+
+
+def collect(coupled, scaled):
+    width, count = scaled[0].shape[2], len(coupled)
 
     def kernel(*refs):
-        coupled, scaled, outs, total = refs[:8], refs[8:-5], refs[-5:-1], refs[-1]
+        coupled, scaled, total = refs[:count], refs[count:-1], refs[-1]
+        total[...] = jnp.zeros_like(total)
+        for n, place in enumerate(places_in(coupled)):
+            total[place] += tdot(coupled[n][pl.ds(0, ROWS)], scaled[n // 2][n % 2])
+
+    return pl.pallas_call(
+        kernel,
+        out_shape=jax.ShapeDtypeStruct((8, TILE, width), F32),
+        in_specs=[VMEM] * (count + len(scaled)),
+        out_specs=VMEM,
+        compiler_params=pltpu.CompilerParams(vmem_limit_bytes=20 << 20),
+        cost_estimate=pl.CostEstimate(flops=1 << 10, bytes_accessed=1 << 10, transcendentals=0),
+        name="collect",
+    )(*coupled, *scaled)
+
+
+def correct(total, coupled, scaled):
+    width = total.shape[2]
+
+    def kernel(total, *refs):
+        coupled, scaled, outs = refs[:2], refs[2:-4], refs[-4:]
         scaled = [ref.at[j] for ref in scaled for j in range(ref.shape[0])]
-        total[...] = jnp.zeros_like(total)
-        tags = sum(tag_of(coupled[2 * d]) * (0.5 * 64**d) for d in range(4))
-        places = jnp.max(tags).astype(jnp.int32)
-        for d in range(4):
-            for j in range(2):
-                place = (places >> (6 * d + 3 * j)) & 7
-                total[place] += tdot(coupled[2 * d + j][pl.ds(0, ROWS)], scaled[2 * d + j][...])
+        places = places_in(coupled)
+        terms = [tdot(coupled[j][pl.ds(0, ROWS)], scaled[j][...]) for j in range(2)]
         for k in range(8):
-            outs[k % 4][k // 4] = total[k].astype(BF)
+            value = total[k]
+            for place, term in zip(places, terms):
+                value = value + jnp.where(place == k, term, 0.0)
+            outs[k % 4][k // 4] = value.astype(BF)
 
     return pl.pallas_call(
         kernel,
         out_shape=[jax.ShapeDtypeStruct((2, TILE, width), BF)] * 4,
-        in_specs=[VMEM] * (8 + len(scaled)),
+        in_specs=[VMEM] * (3 + len(scaled)),
         out_specs=[VMEM] * 4,
-        scratch_shapes=[pltpu.VMEM((8, TILE, width), F32)],
         compiler_params=pltpu.CompilerParams(vmem_limit_bytes=20 << 20),
         cost_estimate=pl.CostEstimate(flops=1 << 10, bytes_accessed=1 << 10, transcendentals=0),
         name="correct",
-    )(*coupled, *scaled)
+    )(total, *coupled, *scaled)
 
 
 def add(a, b):
@@ -183,9 +206,10 @@
     above, below = shift(basis, y=-1), shift(basis, y=1)
     away = couple(1, spot, modes, stiffness)
     came = [shift(piece, c=1) for piece in away]
-    kept = couple(0, spot, modes, stiffness)
+    late, crossed = lax.optimization_barrier((spot, crossed))
+    kept = couple(0, late, modes, stiffness)
     both = [add(*pair) for pair in zip(kept, came)]
-    crossed, *_ = lax.optimization_barrier((crossed, *both))
+    crossed, _ = lax.optimization_barrier((crossed, both[0]))
     cabove, cbelow = shift(crossed, y=-1), shift(crossed, y=1)
     met2, met13, met0 = (shift(item, xh=1) for item in (both[0], jnp.concatenate(both[1:3]), both[3]))
     met2, above, below = lax.optimization_barrier((met2, above, below))
@@ -210,30 +234,30 @@
     (part0,) = project([(own[0], other[0])], tiles)
     swap = (blk & 1) == 1
     lam = jnp.where(swap, eigen[::-1], eigen)[:, :, None]
-    heard = [(shift(part1[h], z=-1), shift(part3[h], z=1)) for h in range(2)]
-    sums, scaled = zip(*[scale(lam, [part0[h], *heard[h]]) for h in range(2)])
-
-    coupled = [item for d in range(4) for item in (own[d], other[d])]
+    coupled = [item for d in (0, 1, 3) for item in (own[d], other[d])]
     columns = []
+    sums = []
+    heard = shift(part1[0], z=-1), shift(part3[0], z=1)
     for h in range(2):
-        piece = scaled[h]
+        mine, piece = scale(lam, [part0[h], *heard])
+        sums.append(mine)
+        up, down = shift(piece, z=1), shift(piece, z=-1)
+        far = [shift(up[:1], z=1), shift(down[1:], z=-1)]
         if h == 0:
-            pieces = [piece] + [shift(piece, z=d) for d in (1, 2, 3)]
+            part1[1], part3[1], _ = lax.optimization_barrier((part1[1], part3[1], up))
+            heard = shift(part1[1], z=-1), shift(part3[1], z=1)
+        else:
             mine = jnp.concatenate(sums, axis=2)
             mine = jnp.where(swap, mine[::-1], mine)
             projection = jnp.pad(mine, ((0, 0), (0, 512 - ROWS), (0, 0)))
-            pieces[2], projection = lax.optimization_barrier((pieces[2], projection))
-            arrived = pieces[1], pieces[3]
-        else:
-            piece, *_ = lax.optimization_barrier((piece, *arrived))
-            up, down = shift(piece, z=1), shift(piece, z=-1)
-            pieces = [piece, up, shift(up[:1], z=1), shift(down[1:], z=-1), down]
-            pieces[0], ahead, behind = lax.optimization_barrier((pieces[0], ahead, behind))
-        terms = correct(coupled, pieces)
+            far[0], projection = lax.optimization_barrier((far[0], projection))
+            piece, ahead, behind = lax.optimization_barrier((piece, ahead, behind))
+        terms = correct(collect(coupled, [piece, up, down]), [own[2], other[2]], far)
         if h == 1:
             *terms, total = lax.optimization_barrier((*terms, total))
             columns.append(total)
         ahead, behind = shift(terms[2][:1], y=1), shift(terms[2][1:], y=-1)
+        ahead, behind, *_ = lax.optimization_barrier((ahead, behind, *heard))
         ahead = jnp.concatenate([add(terms[1][:1], ahead), terms[1][1:]])
         behind = jnp.concatenate([terms[3][:1], add(terms[3][1:], behind)])
         total = terms[0].astype(F32) + shift(ahead, y=1).astype(F32) + shift(behind, y=-1).astype(F32)

time: 178 us -> 172 us (0.966)
  waiting for transfers between devices: 79.3 us -> 65 us
  starting transfers between devices: 61 us -> 67.5 us
    ppermute x44 -> x45, waiting for transfers between devices: 79.3 us -> 65 us  [shift(): return lax.ppermute(value, AXES, pairs)]
    ppermute x44 -> x45, starting transfers between devices: 61 us -> 67.5 us  [shift(): return lax.ppermute(value, AXES, pairs)]
    pallas_call x0 -> x2, Pallas kernels: none -> 5.15 us  [collect(): pl.pallas_call(kernel, out_shape=jax.ShapeDtypeStruct((8, TILE, width), F...]
    pallas_call x2, Pallas kernels: 6.52 us -> 2.31 us  [correct(): pl.pallas_call(kernel, out_shape=[jax.ShapeDtypeStruct((2, TILE, width),...]
    unnamed x42 -> x52, local copies, waits for them, and re-layouts: 8.73 us -> 10.2 us
  transfers between devices with their start and end apart: 44 -> 45, of which waited for: 23 -> 21; matrix products, arithmetic and copies ran while one was open for 3% -> 4% of each run, Pallas kernels for 8% -> 9%
where the time goes in v1:
time: 172 us; the launch traced here: 170 us
  starting transfers between devices  67.5 us (39%)
  waiting for transfers between devices  65 us (38%)
  Pallas kernels  18.5 us (11%)
  local copies, waits for them, and re-layouts  14.5 us (8%)
  other arithmetic  3.25 us (2%)
    ppermute x45, starting transfers between devices, shift(): return lax.ppermute(value, AXES, pairs)  67.5 us
    ppermute x45, waiting for transfers between devices, shift(): return lax.ppermute(value, AXES, pairs)  65 us
    unnamed x52, local copies, waits for them, and re-layouts  10.2 us
    pallas_call x3, Pallas kernels, project(): pl.pallas_call(kernel, out_shape=[jax.ShapeDtypeStruct(shape, BF) for sha...  6.31 us
    pallas_call x2, Pallas kernels, collect(): pl.pallas_call(kernel, out_shape=jax.ShapeDtypeStruct((8, TILE, width), F...  5.15 us
  transfers between devices with their start and end apart: 45, of which 21 were waited for; matrix products, arithmetic and copies ran while one was open for 4% of the time, Pallas kernels for 9%

profile of v1, /device:TPU:0, one launch (start us, length us, event | category | flops | bytes accessed | tf_op | source)
XLA Modules:
  0.0 170.1 jit_solution(10531039496454037922)
XLA Ops:
  0.6 1.7 collective-permute-start
  2.3 0.7 stack.37.spot
  3.0 2.2 %copy-done = bf16[2,512,2048]{2,1,0:T(8,128)(2,1)S(1)} copy-done((bf16[2,512,2048]{2,1,0:T(8,128)(2,1)S(1)}, bf16[2,512,2048]{2,1,0:T(8,128)(2,1)}, u32[]{:S(2)}) %copy-start) | copy-done | bytes 4194328
  5.2 1.2 copy-done.13
  6.5 1.6 couple.3
  8.7 3.0 %collective-permute-start.7 = (bf16[512,512]{1,0:T(8,128)(2,1)S(1)}, bf16[512,512]{1,0:T(8,128)(2,1)S(1)}, u32[]{:S(2)}, u32[]{:S(2)}) collective-permute-start(bf16[512,512]{1,0:T(8,128)(2,1)S(1)} %copy-done.7), channel_id=1, source_target_pairs={{0,48},{1,49},{2,50},{3,51},{4,52},{5,53},{6,54},{7,55},{8,56},{9,... | collective-permute-start | bytes 1572872 | tf_op jit(solution)/shard_map/ppermute | solution.py:30
  11.7 2.7 %collective-permute-done.refs_6_.refs_8_ = bf16[512,512]{1,0:T(8,128)(2,1)S(1)} collective-permute-done((bf16[512,512]{1,0:T(8,128)(2,1)}, bf16[512,512]{1,0:T(8,128)(2,1)S(1)}, u32[]{:S(2)}, u32[]{:S(2)}) %collective-permute-start) | collective-permute-done | bytes 524320 | tf_op jit(solution)/shard_map/ppermute | solution.py:30
  14.4 1.6 couple.2
  16.8 3.4 %collective-permute-start.6 = (bf16[1,416,512]{2,1,0:T(8,128)(2,1)S(1)}, bf16[1,416,512]{2,1,0:T(8,128)(2,1)S(1)}, u32[]{:S(2)}, u32[]{:S(2)}) collective-permute-start(bf16[1,416,512]{2,1,0:T(8,128)(2,1)S(1)} %add_convert_fusion.4), channel_id=1, source_target_pairs={{0,2},{1,3},{2,0},{3,1},{4,6},{5,7},{6,4},{7,5},{8,10},{9,11},{10,... | collective-permute-start | bytes 1277960 | tf_op jit(solution)/shard_map/ppermute | solution.py:30
  20.2 3.1 %collective-permute-start.11 = (bf16[512,512]{1,0:T(8,128)(2,1)S(1)}, bf16[512,512]{1,0:T(8,128)(2,1)S(1)}, u32[]{:S(2)}, u32[]{:S(2)}) collective-permute-start(bf16[512,512]{1,0:T(8,128)(2,1)S(1)} %collective-permute-done.refs_6_.refs_8_), channel_id=1, source_target_pairs={{0,48},{1,49},{2,50},{3,51},{4,52},{5,53},{6,54},{7,55},{8,56},{9,... | collective-permute-start | bytes 1572872 | tf_op jit(solution)/shard_map/ppermute | solution.py:30
  24.2 2.4 %collective-permute-done.8.refs_5_.refs_7_ = bf16[512,512]{1,0:T(8,128)(2,1)S(1)} collective-permute-done((bf16[512,512]{1,0:T(8,128)(2,1)S(1)}, bf16[512,512]{1,0:T(8,128)(2,1)S(1)}, u32[]{:S(2)}, u32[]{:S(2)}) %collective-permute-start.8) | collective-permute-done | bytes 524320 | tf_op jit(solution)/shard_map/ppermute | solution.py:30
  26.5 2.7 %collective-permute-start.4 = (bf16[2,416,512]{2,1,0:T(8,128)(2,1)S(1)}, bf16[2,416,512]{2,1,0:T(8,128)(2,1)S(1)}, u32[]{:S(2)}, u32[]{:S(2)}) collective-permute-start(bf16[2,416,512]{2,1,0:T(8,128)(2,1)S(1)} %pad_maximum_fusion.1), channel_id=1, source_target_pairs={{0,2},{1,3},{2,0},{3,1},{4,6},{5,7},{6,4},{7,5},{8,10},{9,11},{10,... | collective-permute-start | bytes 2555912 | tf_op jit(solution)/shard_map/ppermute | solution.py:30
  29.3 1.4 collective-permute-done.6
  30.7 4.4 %collective-permute-start.9 = (bf16[416,512]{1,0:T(8,128)(2,1)S(1)}, bf16[416,512]{1,0:T(8,128)(2,1)S(1)}, u32[]{:S(2)}, u32[]{:S(2)}) collective-permute-start(bf16[416,512]{1,0:T(8,128)(2,1)S(1)} %fusion.1), channel_id=1, source_target_pairs={{0,8},{1,9},{2,10},{3,11},{4,12},{5,13},{6,14},{7,15},{8,0},{9,1},... | collective-permute-start | bytes 1277960 | tf_op jit(solution)/shard_map/ppermute | solution.py:30
  35.3 3.3 %collective-permute-start.12 = (bf16[2,256,512]{2,1,0:T(8,128)(2,1)S(1)}, bf16[2,256,512]{2,1,0:T(8,128)(2,1)S(1)}, u32[]{:S(2)}, u32[]{:S(2)}) collective-permute-start(bf16[2,256,512]{2,1,0:T(8,128)(2,1)S(1)} %pad_maximum_fusion.2), channel_id=1, source_target_pairs={{0,48},{1,49},{2,50},{3,51},{4,52},{5,53},{6,54},{7,55},{8,56},{9,... | collective-permute-start | bytes 1572872 | tf_op jit(solution)/shard_map/ppermute | solution.py:30
  38.8 4.8 %collective-permute-done.9.refs_0_ = bf16[416,512]{1,0:T(8,128)(2,1)S(1)} collective-permute-done((bf16[416,512]{1,0:T(8,128)(2,1)S(1)}, bf16[416,512]{1,0:T(8,128)(2,1)S(1)}, u32[]{:S(2)}, u32[]{:S(2)}) %collective-permute-start.9) | collective-permute-done | bytes 426016 | tf_op jit(solution)/shard_map/ppermute | solution.py:30
  43.8 3.1 %collective-permute-start.17 = (bf16[1,416,512]{2,1,0:T(8,128)(2,1)S(1)}, bf16[1,416,512]{2,1,0:T(8,128)(2,1)S(1)}, u32[]{:S(2)}, u32[]{:S(2)}) collective-permute-start(bf16[1,416,512]{2,1,0:T(8,128)(2,1)S(1)} %add_convert_fusion.7), channel_id=1, source_target_pairs={{0,2},{1,3},{2,0},{3,1},{4,6},{5,7},{6,4},{7,5},{8,10},{9,11},{10,... | collective-permute-start | bytes 1277960 | tf_op jit(solution)/shard_map/ppermute | solution.py:30
  46.9 1.5 collective-permute-done.4
  48.5 3.6 %collective-permute-done.14 = bf16[2,256,512]{2,1,0:T(8,128)(2,1)S(1)} collective-permute-done((bf16[2,256,512]{2,1,0:T(8,128)(2,1)S(1)}, bf16[2,256,512]{2,1,0:T(8,128)(2,1)S(1)}, u32[]{:S(2)}, u32[]{:S(2)}) %collective-permute-start.14) | collective-permute-done | bytes 524320 | tf_op jit(solution)/shard_map/ppermute | solution.py:30
  52.3 2.0 %collective-permute-start.15 = (bf16[416,512]{1,0:T(8,128)(2,1)S(1)}, bf16[416,512]{1,0:T(8,128)(2,1)S(1)}, u32[]{:S(2)}, u32[]{:S(2)}) collective-permute-start(bf16[416,512]{1,0:T(8,128)(2,1)S(1)} %get-tuple-element.115), channel_id=1, source_target_pairs={{0,4},{1,5},{2,6},{3,7},{4,8},{5,9},{6,10},{7,11},{8,12},{9,13},{1... | collective-permute-start | bytes 1277960 | tf_op jit(solution)/shard_map/ppermute | solution.py:30
  54.3 2.2 %collective-permute-start.16 = (bf16[416,512]{1,0:T(8,128)(2,1)S(1)}, bf16[416,512]{1,0:T(8,128)(2,1)S(1)}, u32[]{:S(2)}, u32[]{:S(2)}) collective-permute-start(bf16[416,512]{1,0:T(8,128)(2,1)S(1)} %get-tuple-element.114), channel_id=1, source_target_pairs={{0,12},{1,13},{2,14},{3,15},{4,0},{5,1},{6,2},{7,3},{8,4},{9,5},{1... | collective-permute-start | bytes 1277960 | tf_op jit(solution)/shard_map/ppermute | solution.py:30
  56.6 1.1 project.3
  57.7 2.0 %collective-permute-start.21 = (bf16[1,416,512]{2,1,0:T(8,128)(2,1)S(1)}, bf16[1,416,512]{2,1,0:T(8,128)(2,1)S(1)}, u32[]{:S(2)}, u32[]{:S(2)}) collective-permute-start(bf16[1,416,512]{2,1,0:T(8,128)(2,1)S(1)} %get-tuple-element.75), channel_id=1, source_target_pairs={{0,12},{1,13},{2,14},{3,15},{4,0},{5,1},{6,2},{7,3},{8,4},{9,5},{1... | collective-permute-start | bytes 1277960 | tf_op jit(solution)/shard_map/ppermute | solution.py:30
  59.8 7.3 %collective-permute-done.15.refs_0_.refs_2_ = bf16[416,512]{1,0:T(8,128)(2,1)S(1)} collective-permute-done((bf16[416,512]{1,0:T(8,128)(2,1)S(1)}, bf16[416,512]{1,0:T(8,128)(2,1)S(1)}, u32[]{:S(2)}, u32[]{:S(2)}) %collective-permute-start.15) | collective-permute-done | bytes 426016 | tf_op jit(solution)/shard_map/ppermute | solution.py:30
  68.0 0.8 slice_bitcast_fusion.3
  68.8 3.9 %collective-permute-done.21.refs_12_ = bf16[1,416,512]{2,1,0:T(8,128)(2,1)S(1)} collective-permute-done((bf16[1,416,512]{2,1,0:T(8,128)(2,1)S(1)}, bf16[1,416,512]{2,1,0:T(8,128)(2,1)S(1)}, u32[]{:S(2)}, u32[]{:S(2)}) %collective-permute-start.21) | collective-permute-done | bytes 426016 | tf_op jit(solution)/shard_map/ppermute | solution.py:30
  73.2 3.0 %project.5 = (bf16[2,400,256]{2,1,0:T(8,128)(2,1)}, bf16[2,400,256]{2,1,0:T(8,128)(2,1)S(1)}, bf16[2,400,256]{2,1,0:T(8,128)(2,1)}, bf16[2,400,256]{2,1,0:T(8,128)(2,1)S(1)}) custom-call(bf16[416,512]{1,0:T(8,128)(2,1)S(1)} %collective-permute-done.15.refs_0_.refs_2_, bf16[400,512]{1,0:T(8,128)(2,1)S(1)} %collective-permute-done.19.refs_1_.refs_3_, ...), custom_call_target="tpu_custom_call" | custom-call | flops 1024 | bytes 1024 | tf_op jit(solution)/shard_map/project/pallas_call | solution.py:113
  76.3 0.7 copy-done.20
  77.0 0.7 copy-done.22
  77.8 3.0 %collective-permute-start.23 = (bf16[2,400,256]{2,1,0:T(8,128)(2,1)}, bf16[2,400,256]{2,1,0:T(8,128)(2,1)}, u32[]{:S(2)}, u32[]{:S(2)}) collective-permute-start(bf16[2,400,256]{2,1,0:T(8,128)(2,1)} %get-tuple-element.84), channel_id=1, source_target_pairs={{0,12},{1,13},{2,14},{3,15},{4,0},{5,1},{6,2},{7,3},{8,4},{9,5},{1... | collective-permute-start | bytes 1228808 | tf_op jit(solution)/shard_map/ppermute | solution.py:30
  80.9 1.0 copy.9.eigen
  82.0 1.0 copy-done.2
  83.0 1.0 copy-done.4
  84.1 1.0 copy-done.6
  85.1 1.0 copy-done.8
  86.1 1.0 copy-done.11
  87.2 2.2 %project.4 = (bf16[2,400,256]{2,1,0:T(8,128)(2,1)S(1)}, bf16[2,400,256]{2,1,0:T(8,128)(2,1)S(1)}) custom-call(bf16[416,512]{1,0:T(8,128)(2,1)S(1)} %bitcast.37, bf16[400,512]{1,0:T(8,128)(2,1)} %collective-permute-done.18.refs_1_, bf16[512,512]{1,0:T(8,128)(2,1)S(1)} %copy-done.8, bf16[512,512]{1,0:T(8,128)(2,1)S(1)} %collective-permute-done.7.refs_3_.refs_5_, ...), custom_call_target="tpu_custom_call" | custom-call | flops 1024 | bytes 1024 | tf_op jit(solution)/shard_map/project/pallas_call | solution.py:113
  89.4 0.9 collective-permute-done.24.third
  90.3 1.3 scale.2
  91.7 3.2 %collective-permute-start.30 = (bf16[2,400,256]{2,1,0:T(8,128)(2,1)S(1)}, bf16[2,400,256]{2,1,0:T(8,128)(2,1)S(1)}, u32[]{:S(2)}, u32[]{:S(2)}) collective-permute-start(bf16[2,400,256]{2,1,0:T(8,128)(2,1)S(1)} %get-tuple-element.86.refs_6_), channel_id=1, source_target_pairs={{0,12},{1,13},{2,14},{3,15},{4,0},{5,1},{6,2},{7,3},{8,4},{9,5},{1... | collective-permute-start | bytes 1228808 | tf_op jit(solution)/shard_map/ppermute | solution.py:30
  94.9 7.5 %collective-permute-done.25.refs_7_ = bf16[2,400,256]{2,1,0:T(8,128)(2,1)S(1)} collective-permute-done((bf16[2,400,256]{2,1,0:T(8,128)(2,1)S(1)}, bf16[2,400,256]{2,1,0:T(8,128)(2,1)S(1)}, u32[]{:S(2)}, u32[]{:S(2)}) %collective-permute-start.25) | collective-permute-done | bytes 409632 | tf_op jit(solution)/shard_map/ppermute | solution.py:30
  102.5 3.4 %collective-permute-start.32 = (bf16[1,400,256]{2,1,0:T(8,128)(2,1)S(1)}, bf16[1,400,256]{2,1,0:T(8,128)(2,1)S(1)}, u32[]{:S(2)}, u32[]{:S(2)}) collective-permute-start(bf16[1,400,256]{2,1,0:T(8,128)(2,1)S(1)} %slice.148), channel_id=1, source_target_pairs={{0,12},{1,13},{2,14},{3,15},{4,0},{5,1},{6,2},{7,3},{8,4},{9,5},{1... | collective-permute-start | bytes 614408 | tf_op jit(solution)/shard_map/ppermute | solution.py:30
  106.4 1.5 collective-permute-start.27
  107.9 2.6 %collect.2.total = f32[8,512,256]{2,1,0:T(8,128)S(1)} custom-call(bf16[416,512]{1,0:T(8,128)(2,1)S(1)} %bitcast.38, bf16[400,512]{1,0:T(8,128)(2,1)} %collective-permute-done.18.refs_1_, bf16[416,512]{1,0:T(8,128)(2,1)S(1)} %collective-permute-done.15.refs_0_.refs_2_, bf16[400,512]{1,0:T(8,128)(2,1)S(1)} %copy-done.17, ...), custom_call_target="tpu_custom_call" | custom-call | flops 1024 | bytes 1024 | tf_op jit(solution)/shard_map/collect/pallas_call | solution.py:161
  110.6 1.2 correct.2
  111.8 3.2 %collective-permute-start.34 = (bf16[1,512,256]{2,1,0:T(8,128)(2,1)S(1)}, bf16[1,512,256]{2,1,0:T(8,128)(2,1)S(1)}, u32[]{:S(2)}, u32[]{:S(2)}) collective-permute-start(bf16[1,512,256]{2,1,0:T(8,128)(2,1)S(1)} %get-tuple-element.118), channel_id=1, source_target_pairs={{0,48},{1,49},{2,50},{3,51},{4,52},{5,53},{6,54},{7,55},{8,56},{9,... | collective-permute-start | bytes 786440 | tf_op jit(solution)/shard_map/ppermute | solution.py:30
  115.6 5.5 %collective-permute-done.33 = bf16[1,512,256]{2,1,0:T(8,128)(2,1)S(1)} collective-permute-done((bf16[1,512,256]{2,1,0:T(8,128)(2,1)S(1)}, bf16[1,512,256]{2,1,0:T(8,128)(2,1)S(1)}, u32[]{:S(2)}, u32[]{:S(2)}) %collective-permute-start.33) | collective-permute-done | bytes 262176 | tf_op jit(solution)/shard_map/ppermute | solution.py:30
  121.0 0.8 collective-permute-done.34
  122.0 3.8 %collective-permute-start.38 = (bf16[2,512,256]{2,1,0:T(8,128)(2,1)S(1)}, bf16[2,512,256]{2,1,0:T(8,128)(2,1)S(1)}, u32[]{:S(2)}, u32[]{:S(2)}) collective-permute-start(bf16[2,512,256]{2,1,0:T(8,128)(2,1)S(1)} %pad_maximum_fusion.5), channel_id=1, source_target_pairs={{0,48},{1,49},{2,50},{3,51},{4,52},{5,53},{6,54},{7,55},{8,56},{9,... | collective-permute-start | bytes 1572872 | tf_op jit(solution)/shard_map/ppermute | solution.py:30
  126.2 3.2 %collective-permute-start.35 = (bf16[2,400,256]{2,1,0:T(8,128)(2,1)S(1)}, bf16[2,400,256]{2,1,0:T(8,128)(2,1)S(1)}, u32[]{:S(2)}, u32[]{:S(2)}) collective-permute-start(bf16[2,400,256]{2,1,0:T(8,128)(2,1)S(1)} %get-tuple-element.98.refs_6_), channel_id=1, source_target_pairs={{0,12},{1,13},{2,14},{3,15},{4,0},{5,1},{6,2},{7,3},{8,4},{9,5},{1... | collective-permute-start | bytes 1228808 | tf_op jit(solution)/shard_map/ppermute | solution.py:30
  129.7 1.0 pad.4
  130.7 4.7 %collective-permute-done.28.refs_7_ = bf16[2,400,256]{2,1,0:T(8,128)(2,1)S(1)} collective-permute-done((bf16[2,400,256]{2,1,0:T(8,128)(2,1)S(1)}, bf16[2,400,256]{2,1,0:T(8,128)(2,1)S(1)}, u32[]{:S(2)}, u32[]{:S(2)}) %collective-permute-start.28) | collective-permute-done | bytes 409632 | tf_op jit(solution)/shard_map/ppermute | solution.py:30
  135.5 3.5 %collective-permute-start.36 = (bf16[1,400,256]{2,1,0:T(8,128)(2,1)S(1)}, bf16[1,400,256]{2,1,0:T(8,128)(2,1)S(1)}, u32[]{:S(2)}, u32[]{:S(2)}) collective-permute-start(bf16[1,400,256]{2,1,0:T(8,128)(2,1)S(1)} %slice.149), channel_id=1, source_target_pairs={{0,12},{1,13},{2,14},{3,15},{4,0},{5,1},{6,2},{7,3},{8,4},{9,5},{1... | collective-permute-start | bytes 614408 | tf_op jit(solution)/shard_map/ppermute | solution.py:30
  139.0 2.6 %collect.3.total = f32[8,512,256]{2,1,0:T(8,128)S(1)} custom-call(bf16[416,512]{1,0:T(8,128)(2,1)S(1)} %bitcast.39, bf16[400,512]{1,0:T(8,128)(2,1)} %collective-permute-done.18.refs_1_, bf16[416,512]{1,0:T(8,128)(2,1)S(1)} %collective-permute-done.15.refs_0_.refs_2_, bf16[400,512]{1,0:T(8,128)(2,1)S(1)} %copy-done.17, ...), custom_call_target="tpu_custom_call" | custom-call | flops 1024 | bytes 1024 | tf_op jit(solution)/shard_map/collect/pallas_call | solution.py:161
  142.4 1.2 correct.3
  143.7 3.3 %collective-permute-start.41 = (bf16[1,512,256]{2,1,0:T(8,128)(2,1)S(1)}, bf16[1,512,256]{2,1,0:T(8,128)(2,1)S(1)}, u32[]{:S(2)}, u32[]{:S(2)}) collective-permute-start(bf16[1,512,256]{2,1,0:T(8,128)(2,1)S(1)} %get-tuple-element.116), channel_id=1, source_target_pairs={{0,48},{1,49},{2,50},{3,51},{4,52},{5,53},{6,54},{7,55},{8,56},{9,... | collective-permute-start | bytes 786440 | tf_op jit(solution)/shard_map/ppermute | solution.py:30
  147.1 4.3 %collective-permute-done.40 = bf16[1,512,256]{2,1,0:T(8,128)(2,1)S(1)} collective-permute-done((bf16[1,512,256]{2,1,0:T(8,128)(2,1)S(1)}, bf16[1,512,256]{2,1,0:T(8,128)(2,1)S(1)}, u32[]{:S(2)}, u32[]{:S(2)}) %collective-permute-start.40) | collective-permute-done | bytes 262176 | tf_op jit(solution)/shard_map/ppermute | solution.py:30
  151.5 1.4 collective-permute-start.42
  153.0 2.0 %collective-permute-start.43 = (bf16[2,512,256]{2,1,0:T(8,128)(2,1)S(1)}, bf16[2,512,256]{2,1,0:T(8,128)(2,1)S(1)}, u32[]{:S(2)}, u32[]{:S(2)}) collective-permute-start(bf16[2,512,256]{2,1,0:T(8,128)(2,1)S(1)} %pad_maximum_fusion.7), channel_id=1, source_target_pairs={{0,48},{1,49},{2,50},{3,51},{4,52},{5,53},{6,54},{7,55},{8,56},{9,... | collective-permute-start | bytes 1572872 | tf_op jit(solution)/shard_map/ppermute | solution.py:30
  155.0 0.7 collective-permute-start.39
  155.7 6.2 %collective-permute-done.42 = bf16[2,512,256]{2,1,0:T(8,128)(2,1)S(1)} collective-permute-done((bf16[2,512,256]{2,1,0:T(8,128)(2,1)S(1)}, bf16[2,512,256]{2,1,0:T(8,128)(2,1)S(1)}, u32[]{:S(2)}, u32[]{:S(2)}) %collective-permute-start.42) | collective-permute-done | bytes 524320 | tf_op jit(solution)/shard_map/ppermute | solution.py:30
  162.5 0.7 collective-permute-start.44
  163.2 5.7 %collective-permute-done.44 = bf16[512,256]{1,0:T(8,128)(2,1)S(1)} collective-permute-done((bf16[512,256]{1,0:T(8,128)(2,1)S(1)}, bf16[512,256]{1,0:T(8,128)(2,1)S(1)}, u32[]{:S(2)}, u32[]{:S(2)}) %collective-permute-start.44) | collective-permute-done | bytes 262176 | tf_op jit(solution)/shard_map/ppermute | solution.py:30
  169.0 1.1 pad_maximum_fusion
  (141 shorter events, 8.9 us)
Async XLA Ops:
  0.6 13.8 %collective-permute-start = (bf16[512,512]{1,0:T(8,128)(2,1)}, bf16[512,512]{1,0:T(8,128)(2,1)S(1)}, u32[]{:S(2)}, u32[]{:S(2)}) collective-permute-start(bf16[512,512]{1,0:T(8,128)(2,1)} %refs_4_.1), channel_id=1, source_target_pairs={{0,64},{1,65},{2,66},{3,67},{4,68},{5,69},{6,70},{7,71},{8,72},{9,... | collective-permute-start | bytes 1572872 | tf_op jit(solution)/shard_map/ppermute | solution.py:30
  3.0 2.2 %copy-start = (bf16[2,512,2048]{2,1,0:T(8,128)(2,1)S(1)}, bf16[2,512,2048]{2,1,0:T(8,128)(2,1)}, u32[]{:S(2)}) copy-start(bf16[2,512,2048]{2,1,0:T(8,128)(2,1)} %stiffness.3) | copy-start | bytes 12582916
  5.2 1.2 copy-start.13
  6.4 2.2 %copy-start.7 = (bf16[512,512]{1,0:T(8,128)(2,1)S(1)}, bf16[512,512]{1,0:T(8,128)(2,1)}, u32[]{:S(2)}) copy-start(bf16[512,512]{1,0:T(8,128)(2,1)} %refs_4_.1) | copy-start | bytes 1572868
  8.1 8.0 %collective-permute-start.5 = (bf16[1,416,512]{2,1,0:T(8,128)(2,1)S(1)}, bf16[1,416,512]{2,1,0:T(8,128)(2,1)S(1)}, u32[]{:S(2)}, u32[]{:S(2)}) collective-permute-start(bf16[1,416,512]{2,1,0:T(8,128)(2,1)S(1)} %get-tuple-element.65), channel_id=1, source_target_pairs={{0,1},{1,0},{2,3},{3,2},{4,5},{5,4},{6,7},{7,6},{8,9},{9,8},{10,11... | collective-permute-start | bytes 1277960 | tf_op jit(solution)/shard_map/ppermute | solution.py:30
  8.2 8.6 %collective-permute-start.3 = (bf16[1,416,512]{2,1,0:T(8,128)(2,1)S(1)}, bf16[1,416,512]{2,1,0:T(8,128)(2,1)S(1)}, u32[]{:S(2)}, u32[]{:S(2)}) collective-permute-start(bf16[1,416,512]{2,1,0:T(8,128)(2,1)S(1)} %get-tuple-element.63), channel_id=1, source_target_pairs={{0,1},{1,0},{2,3},{3,2},{4,5},{5,4},{6,7},{7,6},{8,9},{9,8},{10,11... | collective-permute-start | bytes 1277960 | tf_op jit(solution)/shard_map/ppermute | solution.py:30
  8.7 14.9 %collective-permute-start.7 = (bf16[512,512]{1,0:T(8,128)(2,1)S(1)}, bf16[512,512]{1,0:T(8,128)(2,1)S(1)}, u32[]{:S(2)}, u32[]{:S(2)}) collective-permute-start(bf16[512,512]{1,0:T(8,128)(2,1)S(1)} %copy-done.7), channel_id=1, source_target_pairs={{0,48},{1,49},{2,50},{3,51},{4,52},{5,53},{6,54},{7,55},{8,56},{9,... | collective-permute-start | bytes 1572872 | tf_op jit(solution)/shard_map/ppermute | solution.py:30
  11.7 14.9 %collective-permute-start.8 = (bf16[512,512]{1,0:T(8,128)(2,1)S(1)}, bf16[512,512]{1,0:T(8,128)(2,1)S(1)}, u32[]{:S(2)}, u32[]{:S(2)}) collective-permute-start(bf16[512,512]{1,0:T(8,128)(2,1)S(1)} %copy-done.7), channel_id=1, source_target_pairs={{0,16},{1,17},{2,18},{3,19},{4,20},{5,21},{6,22},{7,23},{8,24},{9,... | collective-permute-start | bytes 1572872 | tf_op jit(solution)/shard_map/ppermute | solution.py:30
  14.4 9.1 %copy-start.9 = (bf16[512,512]{1,0:T(8,128)(2,1)}, bf16[512,512]{1,0:T(8,128)(2,1)S(1)}, u32[]{:S(2)}) copy-start(bf16[512,512]{1,0:T(8,128)(2,1)S(1)} %collective-permute-done.refs_6_.refs_8_) | copy-start | bytes 1572868
  14.4 5.8 %collective-permute-start.2 = (bf16[1,416,512]{2,1,0:T(8,128)(2,1)S(1)}, bf16[1,416,512]{2,1,0:T(8,128)(2,1)S(1)}, u32[]{:S(2)}, u32[]{:S(2)}) collective-permute-start(bf16[1,416,512]{2,1,0:T(8,128)(2,1)S(1)} %get-tuple-element.61), channel_id=1, source_target_pairs={{0,1},{1,0},{2,3},{3,2},{4,5},{5,4},{6,7},{7,6},{8,9},{9,8},{10,11... | collective-permute-start | bytes 1277960 | tf_op jit(solution)/shard_map/ppermute | solution.py:30
  16.1 27.6 %collective-permute-start.1 = (bf16[1,416,512]{2,1,0:T(8,128)(2,1)S(1)}, bf16[1,416,512]{2,1,0:T(8,128)(2,1)S(1)}, u32[]{:S(2)}, u32[]{:S(2)}) collective-permute-start(bf16[1,416,512]{2,1,0:T(8,128)(2,1)S(1)} %get-tuple-element.59), channel_id=1, source_target_pairs={{0,1},{1,0},{2,3},{3,2},{4,5},{5,4},{6,7},{7,6},{8,9},{9,8},{10,11... | collective-permute-start | bytes 1277960 | tf_op jit(solution)/shard_map/ppermute | solution.py:30
  16.8 13.9 %collective-permute-start.6 = (bf16[1,416,512]{2,1,0:T(8,128)(2,1)S(1)}, bf16[1,416,512]{2,1,0:T(8,128)(2,1)S(1)}, u32[]{:S(2)}, u32[]{:S(2)}) collective-permute-start(bf16[1,416,512]{2,1,0:T(8,128)(2,1)S(1)} %add_convert_fusion.4), channel_id=1, source_target_pairs={{0,2},{1,3},{2,0},{3,1},{4,6},{5,7},{6,4},{7,5},{8,10},{9,11},{10,... | collective-permute-start | bytes 1277960 | tf_op jit(solution)/shard_map/ppermute | solution.py:30
  20.2 14.9 %collective-permute-start.11 = (bf16[512,512]{1,0:T(8,128)(2,1)S(1)}, bf16[512,512]{1,0:T(8,128)(2,1)S(1)}, u32[]{:S(2)}, u32[]{:S(2)}) collective-permute-start(bf16[512,512]{1,0:T(8,128)(2,1)S(1)} %collective-permute-done.refs_6_.refs_8_), channel_id=1, source_target_pairs={{0,48},{1,49},{2,50},{3,51},{4,52},{5,53},{6,54},{7,55},{8,56},{9,... | collective-permute-start | bytes 1572872 | tf_op jit(solution)/shard_map/ppermute | solution.py:30
  23.5 15.1 %collective-permute-start.13 = (bf16[512,512]{1,0:T(8,128)(2,1)S(1)}, bf16[512,512]{1,0:T(8,128)(2,1)S(1)}, u32[]{:S(2)}, u32[]{:S(2)}) collective-permute-start(bf16[512,512]{1,0:T(8,128)(2,1)S(1)} %collective-permute-done.refs_6_.refs_8_), channel_id=1, source_target_pairs={{0,16},{1,17},{2,18},{3,19},{4,20},{5,21},{6,22},{7,23},{8,24},{9,... | collective-permute-start | bytes 1572872 | tf_op jit(solution)/shard_map/ppermute | solution.py:30
  26.5 46.6 %copy-start.1 = (bf16[512,512]{1,0:T(8,128)(2,1)}, bf16[512,512]{1,0:T(8,128)(2,1)S(1)}, u32[]{:S(2)}) copy-start(bf16[512,512]{1,0:T(8,128)(2,1)S(1)} %collective-permute-done.8.refs_5_.refs_7_) | copy-start | bytes 1572868
  26.5 21.9 %collective-permute-start.4 = (bf16[2,416,512]{2,1,0:T(8,128)(2,1)S(1)}, bf16[2,416,512]{2,1,0:T(8,128)(2,1)S(1)}, u32[]{:S(2)}, u32[]{:S(2)}) collective-permute-start(bf16[2,416,512]{2,1,0:T(8,128)(2,1)S(1)} %pad_maximum_fusion.1), channel_id=1, source_target_pairs={{0,2},{1,3},{2,0},{3,1},{4,6},{5,7},{6,4},{7,5},{8,10},{9,11},{10,... | collective-permute-start | bytes 2555912 | tf_op jit(solution)/shard_map/ppermute | solution.py:30
  30.7 12.8 %collective-permute-start.9 = (bf16[416,512]{1,0:T(8,128)(2,1)S(1)}, bf16[416,512]{1,0:T(8,128)(2,1)S(1)}, u32[]{:S(2)}, u32[]{:S(2)}) collective-permute-start(bf16[416,512]{1,0:T(8,128)(2,1)S(1)} %fusion.1), channel_id=1, source_target_pairs={{0,8},{1,9},{2,10},{3,11},{4,12},{5,13},{6,14},{7,15},{8,0},{9,1},... | collective-permute-start | bytes 1277960 | tf_op jit(solution)/shard_map/ppermute | solution.py:30
  35.2 38.0 %copy-start.3 = (bf16[512,512]{1,0:T(8,128)(2,1)}, bf16[512,512]{1,0:T(8,128)(2,1)S(1)}, u32[]{:S(2)}) copy-start(bf16[512,512]{1,0:T(8,128)(2,1)S(1)} %collective-permute-done.11.refs_7_.refs_9_) | copy-start | bytes 1572868
  35.3 13.2 %collective-permute-start.12 = (bf16[2,256,512]{2,1,0:T(8,128)(2,1)S(1)}, bf16[2,256,512]{2,1,0:T(8,128)(2,1)S(1)}, u32[]{:S(2)}, u32[]{:S(2)}) collective-permute-start(bf16[2,256,512]{2,1,0:T(8,128)(2,1)S(1)} %pad_maximum_fusion.2), channel_id=1, source_target_pairs={{0,48},{1,49},{2,50},{3,51},{4,52},{5,53},{6,54},{7,55},{8,56},{9,... | collective-permute-start | bytes 1572872 | tf_op jit(solution)/shard_map/ppermute | solution.py:30
  38.6 34.6 %copy-start.5 = (bf16[512,512]{1,0:T(8,128)(2,1)}, bf16[512,512]{1,0:T(8,128)(2,1)S(1)}, u32[]{:S(2)}) copy-start(bf16[512,512]{1,0:T(8,128)(2,1)S(1)} %collective-permute-done.13.refs_9_.refs_11_) | copy-start | bytes 1572868
  38.7 13.3 %collective-permute-start.14 = (bf16[2,256,512]{2,1,0:T(8,128)(2,1)S(1)}, bf16[2,256,512]{2,1,0:T(8,128)(2,1)S(1)}, u32[]{:S(2)}, u32[]{:S(2)}) collective-permute-start(bf16[2,256,512]{2,1,0:T(8,128)(2,1)S(1)} %pad_maximum_fusion.3), channel_id=1, source_target_pairs={{0,16},{1,17},{2,18},{3,19},{4,20},{5,21},{6,22},{7,23},{8,24},{9,... | collective-permute-start | bytes 1572872 | tf_op jit(solution)/shard_map/ppermute | solution.py:30
  43.6 13.0 %copy-start.10 = (bf16[512,512]{1,0:T(8,128)(2,1)S(1)}, bf16[512,512]{1,0:T(8,128)(2,1)}, u32[]{:S(2)}) copy-start(bf16[512,512]{1,0:T(8,128)(2,1)} %copy-done.9) | copy-start | bytes 1572868
  43.6 8.4 %collective-permute-start.10 = (bf16[400,512]{1,0:T(8,128)(2,1)S(1)}, bf16[400,512]{1,0:T(8,128)(2,1)S(1)}, u32[]{:S(2)}, u32[]{:S(2)}) collective-permute-start(bf16[400,512]{1,0:T(8,128)(2,1)S(1)} %slice.140), channel_id=1, source_target_pairs={{0,1},{1,0},{2,3},{3,2},{4,5},{5,4},{6,7},{7,6},{8,9},{9,8},{10,11... | collective-permute-start | bytes 1228808 | tf_op jit(solution)/shard_map/ppermute | solution.py:30
  43.8 16.0 %collective-permute-start.17 = (bf16[1,416,512]{2,1,0:T(8,128)(2,1)S(1)}, bf16[1,416,512]{2,1,0:T(8,128)(2,1)S(1)}, u32[]{:S(2)}, u32[]{:S(2)}) collective-permute-start(bf16[1,416,512]{2,1,0:T(8,128)(2,1)S(1)} %add_convert_fusion.7), channel_id=1, source_target_pairs={{0,2},{1,3},{2,0},{3,1},{4,6},{5,7},{6,4},{7,5},{8,10},{9,11},{10,... | collective-permute-start | bytes 1277960 | tf_op jit(solution)/shard_map/ppermute | solution.py:30
  52.0 5.7 %copy-start.14 = (bf16[400,512]{1,0:T(8,128)(2,1)}, bf16[400,512]{1,0:T(8,128)(2,1)S(1)}, u32[]{:S(2)}) copy-start(bf16[400,512]{1,0:T(8,128)(2,1)S(1)} %collective-permute-done.10.refs_1_) | copy-start | bytes 1228804
  52.3 14.8 %collective-permute-start.15 = (bf16[416,512]{1,0:T(8,128)(2,1)S(1)}, bf16[416,512]{1,0:T(8,128)(2,1)S(1)}, u32[]{:S(2)}, u32[]{:S(2)}) collective-permute-start(bf16[416,512]{1,0:T(8,128)(2,1)S(1)} %get-tuple-element.115), channel_id=1, source_target_pairs={{0,4},{1,5},{2,6},{3,7},{4,8},{5,9},{6,10},{7,11},{8,12},{9,13},{1... | collective-permute-start | bytes 1277960 | tf_op jit(solution)/shard_map/ppermute | solution.py:30
  54.3 12.9 %collective-permute-start.16 = (bf16[416,512]{1,0:T(8,128)(2,1)S(1)}, bf16[416,512]{1,0:T(8,128)(2,1)S(1)}, u32[]{:S(2)}, u32[]{:S(2)}) collective-permute-start(bf16[416,512]{1,0:T(8,128)(2,1)S(1)} %get-tuple-element.114), channel_id=1, source_target_pairs={{0,12},{1,13},{2,14},{3,15},{4,0},{5,1},{6,2},{7,3},{8,4},{9,5},{1... | collective-permute-start | bytes 1277960 | tf_op jit(solution)/shard_map/ppermute | solution.py:30
  57.7 15.0 %collective-permute-start.21 = (bf16[1,416,512]{2,1,0:T(8,128)(2,1)S(1)}, bf16[1,416,512]{2,1,0:T(8,128)(2,1)S(1)}, u32[]{:S(2)}, u32[]{:S(2)}) collective-permute-start(bf16[1,416,512]{2,1,0:T(8,128)(2,1)S(1)} %get-tuple-element.75), channel_id=1, source_target_pairs={{0,12},{1,13},{2,14},{3,15},{4,0},{5,1},{6,2},{7,3},{8,4},{9,5},{1... | collective-permute-start | bytes 1277960 | tf_op jit(solution)/shard_map/ppermute | solution.py:30
  59.7 13.4 %collective-permute-start.22 = (bf16[1,416,512]{2,1,0:T(8,128)(2,1)S(1)}, bf16[1,416,512]{2,1,0:T(8,128)(2,1)S(1)}, u32[]{:S(2)}, u32[]{:S(2)}) collective-permute-start(bf16[1,416,512]{2,1,0:T(8,128)(2,1)S(1)} %get-tuple-element.80), channel_id=1, source_target_pairs={{0,4},{1,5},{2,6},{3,7},{4,8},{5,9},{6,10},{7,11},{8,12},{9,13},{1... | collective-permute-start | bytes 1277960 | tf_op jit(solution)/shard_map/ppermute | solution.py:30
  67.1 6.0 %collective-permute-start.19 = (bf16[400,512]{1,0:T(8,128)(2,1)S(1)}, bf16[400,512]{1,0:T(8,128)(2,1)S(1)}, u32[]{:S(2)}, u32[]{:S(2)}) collective-permute-start(bf16[400,512]{1,0:T(8,128)(2,1)S(1)} %slice.118), channel_id=1, source_target_pairs={{0,1},{1,0},{2,3},{3,2},{4,5},{5,4},{6,7},{7,6},{8,9},{9,8},{10,11... | collective-permute-start | bytes 1228808 | tf_op jit(solution)/shard_map/ppermute | solution.py:30
  67.3 13.5 %copy-start.24 = (f32[2,512]{1,0:T(2,128)S(1)}, f32[2,512]{1,0:T(2,128)}, u32[]{:S(2)}) copy-start(f32[2,512]{1,0:T(2,128)} %param.9) | copy-start | bytes 12292
  67.3 5.9 %collective-permute-start.20 = (bf16[400,512]{1,0:T(8,128)(2,1)S(1)}, bf16[400,512]{1,0:T(8,128)(2,1)S(1)}, u32[]{:S(2)}, u32[]{:S(2)}) collective-permute-start(bf16[400,512]{1,0:T(8,128)(2,1)S(1)} %slice.119), channel_id=1, source_target_pairs={{0,1},{1,0},{2,3},{3,2},{4,5},{5,4},{6,7},{7,6},{8,9},{9,8},{10,11... | collective-permute-start | bytes 1228808 | tf_op jit(solution)/shard_map/ppermute | solution.py:30
  68.8 13.2 %collective-permute-start.18 = (bf16[400,512]{1,0:T(8,128)(2,1)}, bf16[400,512]{1,0:T(8,128)(2,1)}, u32[]{:S(2)}, u32[]{:S(2)}) collective-permute-start(bf16[400,512]{1,0:T(8,128)(2,1)} %slice_bitcast_fusion.3), channel_id=1, source_target_pairs={{0,1},{1,0},{2,3},{3,2},{4,5},{5,4},{6,7},{7,6},{8,9},{9,8},{10,11... | collective-permute-start | bytes 1228808 | tf_op jit(solution)/shard_map/ppermute | solution.py:30
  73.1 3.1 %copy-start.16 = (bf16[400,512]{1,0:T(8,128)(2,1)}, bf16[400,512]{1,0:T(8,128)(2,1)S(1)}, u32[]{:S(2)}) copy-start(bf16[400,512]{1,0:T(8,128)(2,1)S(1)} %collective-permute-done.19.refs_1_.refs_3_) | copy-start | bytes 1228804
  73.2 4.6 %copy-start.18 = (bf16[400,512]{1,0:T(8,128)(2,1)}, bf16[400,512]{1,0:T(8,128)(2,1)S(1)}, u32[]{:S(2)}) copy-start(bf16[400,512]{1,0:T(8,128)(2,1)S(1)} %collective-permute-done.20.refs_3_.refs_5_) | copy-start | bytes 1228804
  77.8 11.6 %collective-permute-start.23 = (bf16[2,400,256]{2,1,0:T(8,128)(2,1)}, bf16[2,400,256]{2,1,0:T(8,128)(2,1)}, u32[]{:S(2)}, u32[]{:S(2)}) collective-permute-start(bf16[2,400,256]{2,1,0:T(8,128)(2,1)} %get-tuple-element.84), channel_id=1, source_target_pairs={{0,12},{1,13},{2,14},{3,15},{4,0},{5,1},{6,2},{7,3},{8,4},{9,5},{1... | collective-permute-start | bytes 1228808 | tf_op jit(solution)/shard_map/ppermute | solution.py:30
  80.8 9.5 %collective-permute-start.24 = (bf16[2,400,256]{2,1,0:T(8,128)(2,1)}, bf16[2,400,256]{2,1,0:T(8,128)(2,1)}, u32[]{:S(2)}, u32[]{:S(2)}) collective-permute-start(bf16[2,400,256]{2,1,0:T(8,128)(2,1)} %get-tuple-element.85), channel_id=1, source_target_pairs={{0,4},{1,5},{2,6},{3,7},{4,8},{5,9},{6,10},{7,11},{8,12},{9,13},{1... | collective-permute-start | bytes 1228808 | tf_op jit(solution)/shard_map/ppermute | solution.py:30
  82.0 1.0 copy-start.2
  87.2 3.1 %copy-start.12 = (f32[2,512,1]{2,1,0:T(8,128)S(1)}, f32[2,512,1]{2,1,0:T(8,128)}, u32[]{:S(2)}) copy-start(f32[2,512,1]{2,1,0:T(8,128)} %copy.9.eigen) | copy-start | bytes 12292
  87.2 18.7 %copy-start.23 = (bf16[2,400,256]{2,1,0:T(8,128)(2,1)S(1)}, bf16[2,400,256]{2,1,0:T(8,128)(2,1)}, u32[]{:S(2)}) copy-start(bf16[2,400,256]{2,1,0:T(8,128)(2,1)} %copy-done.22) | copy-start | bytes 1228804
  87.2 19.2 %copy-start.21 = (bf16[2,400,256]{2,1,0:T(8,128)(2,1)S(1)}, bf16[2,400,256]{2,1,0:T(8,128)(2,1)}, u32[]{:S(2)}) copy-start(bf16[2,400,256]{2,1,0:T(8,128)(2,1)} %copy-done.20) | copy-start | bytes 1228804
  87.2 20.8 %copy-start.17 = (bf16[400,512]{1,0:T(8,128)(2,1)S(1)}, bf16[400,512]{1,0:T(8,128)(2,1)}, u32[]{:S(2)}) copy-start(bf16[400,512]{1,0:T(8,128)(2,1)} %copy-done.16) | copy-start | bytes 1228804
  87.2 20.8 %copy-start.19 = (bf16[400,512]{1,0:T(8,128)(2,1)S(1)}, bf16[400,512]{1,0:T(8,128)(2,1)}, u32[]{:S(2)}) copy-start(bf16[400,512]{1,0:T(8,128)(2,1)} %copy-done.18) | copy-start | bytes 1228804
  91.6 10.8 %collective-permute-start.25 = (bf16[2,400,256]{2,1,0:T(8,128)(2,1)S(1)}, bf16[2,400,256]{2,1,0:T(8,128)(2,1)S(1)}, u32[]{:S(2)}, u32[]{:S(2)}) collective-permute-start(bf16[2,400,256]{2,1,0:T(8,128)(2,1)S(1)} %get-tuple-element.86.refs_6_), channel_id=1, source_target_pairs={{0,4},{1,5},{2,6},{3,7},{4,8},{5,9},{6,10},{7,11},{8,12},{9,13},{1... | collective-permute-start | bytes 1228808 | tf_op jit(solution)/shard_map/ppermute | solution.py:30
  91.7 10.8 %collective-permute-start.30 = (bf16[2,400,256]{2,1,0:T(8,128)(2,1)S(1)}, bf16[2,400,256]{2,1,0:T(8,128)(2,1)S(1)}, u32[]{:S(2)}, u32[]{:S(2)}) collective-permute-start(bf16[2,400,256]{2,1,0:T(8,128)(2,1)S(1)} %get-tuple-element.86.refs_6_), channel_id=1, source_target_pairs={{0,12},{1,13},{2,14},{3,15},{4,0},{5,1},{6,2},{7,3},{8,4},{9,5},{1... | collective-permute-start | bytes 1228808 | tf_op jit(solution)/shard_map/ppermute | solution.py:30
  102.4 8.1 %copy-start.15 = (bf16[400,512]{1,0:T(8,128)(2,1)S(1)}, bf16[400,512]{1,0:T(8,128)(2,1)}, u32[]{:S(2)}) copy-start(bf16[400,512]{1,0:T(8,128)(2,1)} %copy-done.14) | copy-start | bytes 1228804
  102.4 8.1 %collective-permute-start.31 = (bf16[1,400,256]{2,1,0:T(8,128)(2,1)S(1)}, bf16[1,400,256]{2,1,0:T(8,128)(2,1)S(1)}, u32[]{:S(2)}, u32[]{:S(2)}) collective-permute-start(bf16[1,400,256]{2,1,0:T(8,128)(2,1)S(1)} %slice.147), channel_id=1, source_target_pairs={{0,4},{1,5},{2,6},{3,7},{4,8},{5,9},{6,10},{7,11},{8,12},{9,13},{1... | collective-permute-start | bytes 614408 | tf_op jit(solution)/shard_map/ppermute | solution.py:30
  102.5 8.0 %collective-permute-start.32 = (bf16[1,400,256]{2,1,0:T(8,128)(2,1)S(1)}, bf16[1,400,256]{2,1,0:T(8,128)(2,1)S(1)}, u32[]{:S(2)}, u32[]{:S(2)}) collective-permute-start(bf16[1,400,256]{2,1,0:T(8,128)(2,1)S(1)} %slice.148), channel_id=1, source_target_pairs={{0,12},{1,13},{2,14},{3,15},{4,0},{5,1},{6,2},{7,3},{8,4},{9,5},{1... | collective-permute-start | bytes 614408 | tf_op jit(solution)/shard_map/ppermute | solution.py:30
  105.9 9.2 %collective-permute-start.26 = (bf16[2,400,256]{2,1,0:T(8,128)(2,1)S(1)}, bf16[2,400,256]{2,1,0:T(8,128)(2,1)S(1)}, u32[]{:S(2)}, u32[]{:S(2)}) collective-permute-start(bf16[2,400,256]{2,1,0:T(8,128)(2,1)S(1)} %copy-done.23), channel_id=1, source_target_pairs={{0,12},{1,13},{2,14},{3,15},{4,0},{5,1},{6,2},{7,3},{8,4},{9,5},{1... | collective-permute-start | bytes 1228808 | tf_op jit(solution)/shard_map/ppermute | solution.py:30
  106.4 9.2 %collective-permute-start.27 = (bf16[2,400,256]{2,1,0:T(8,128)(2,1)S(1)}, bf16[2,400,256]{2,1,0:T(8,128)(2,1)S(1)}, u32[]{:S(2)}, u32[]{:S(2)}) collective-permute-start(bf16[2,400,256]{2,1,0:T(8,128)(2,1)S(1)} %copy-done.21), channel_id=1, source_target_pairs={{0,4},{1,5},{2,6},{3,7},{4,8},{5,9},{6,10},{7,11},{8,12},{9,13},{1... | collective-permute-start | bytes 1228808 | tf_op jit(solution)/shard_map/ppermute | solution.py:30
  111.8 9.3 %collective-permute-start.33 = (bf16[1,512,256]{2,1,0:T(8,128)(2,1)S(1)}, bf16[1,512,256]{2,1,0:T(8,128)(2,1)S(1)}, u32[]{:S(2)}, u32[]{:S(2)}) collective-permute-start(bf16[1,512,256]{2,1,0:T(8,128)(2,1)S(1)} %get-tuple-element.119), channel_id=1, source_target_pairs={{0,16},{1,17},{2,18},{3,19},{4,20},{5,21},{6,22},{7,23},{8,24},{9,... | collective-permute-start | bytes 786440 | tf_op jit(solution)/shard_map/ppermute | solution.py:30
  111.8 10.0 %collective-permute-start.34 = (bf16[1,512,256]{2,1,0:T(8,128)(2,1)S(1)}, bf16[1,512,256]{2,1,0:T(8,128)(2,1)S(1)}, u32[]{:S(2)}, u32[]{:S(2)}) collective-permute-start(bf16[1,512,256]{2,1,0:T(8,128)(2,1)S(1)} %get-tuple-element.118), channel_id=1, source_target_pairs={{0,48},{1,49},{2,50},{3,51},{4,52},{5,53},{6,54},{7,55},{8,56},{9,... | collective-permute-start | bytes 786440 | tf_op jit(solution)/shard_map/ppermute | solution.py:30
  122.0 19.6 %collective-permute-start.38 = (bf16[2,512,256]{2,1,0:T(8,128)(2,1)S(1)}, bf16[2,512,256]{2,1,0:T(8,128)(2,1)S(1)}, u32[]{:S(2)}, u32[]{:S(2)}) collective-permute-start(bf16[2,512,256]{2,1,0:T(8,128)(2,1)S(1)} %pad_maximum_fusion.5), channel_id=1, source_target_pairs={{0,48},{1,49},{2,50},{3,51},{4,52},{5,53},{6,54},{7,55},{8,56},{9,... | collective-permute-start | bytes 1572872 | tf_op jit(solution)/shard_map/ppermute | solution.py:30
  125.8 15.8 %collective-permute-start.37 = (bf16[2,512,256]{2,1,0:T(8,128)(2,1)S(1)}, bf16[2,512,256]{2,1,0:T(8,128)(2,1)S(1)}, u32[]{:S(2)}, u32[]{:S(2)}) collective-permute-start(bf16[2,512,256]{2,1,0:T(8,128)(2,1)S(1)} %pad_maximum_fusion.4), channel_id=1, source_target_pairs={{0,16},{1,17},{2,18},{3,19},{4,20},{5,21},{6,22},{7,23},{8,24},{9,... | collective-permute-start | bytes 1572872 | tf_op jit(solution)/shard_map/ppermute | solution.py:30
  126.1 9.2 %collective-permute-start.28 = (bf16[2,400,256]{2,1,0:T(8,128)(2,1)S(1)}, bf16[2,400,256]{2,1,0:T(8,128)(2,1)S(1)}, u32[]{:S(2)}, u32[]{:S(2)}) collective-permute-start(bf16[2,400,256]{2,1,0:T(8,128)(2,1)S(1)} %get-tuple-element.98.refs_6_), channel_id=1, source_target_pairs={{0,4},{1,5},{2,6},{3,7},{4,8},{5,9},{6,10},{7,11},{8,12},{9,13},{1... | collective-permute-start | bytes 1228808 | tf_op jit(solution)/shard_map/ppermute | solution.py:30
  126.2 9.3 %collective-permute-start.35 = (bf16[2,400,256]{2,1,0:T(8,128)(2,1)S(1)}, bf16[2,400,256]{2,1,0:T(8,128)(2,1)S(1)}, u32[]{:S(2)}, u32[]{:S(2)}) collective-permute-start(bf16[2,400,256]{2,1,0:T(8,128)(2,1)S(1)} %get-tuple-element.98.refs_6_), channel_id=1, source_target_pairs={{0,12},{1,13},{2,14},{3,15},{4,0},{5,1},{6,2},{7,3},{8,4},{9,5},{1... | collective-permute-start | bytes 1228808 | tf_op jit(solution)/shard_map/ppermute | solution.py:30
  135.4 7.0 %collective-permute-start.29 = (bf16[1,400,256]{2,1,0:T(8,128)(2,1)S(1)}, bf16[1,400,256]{2,1,0:T(8,128)(2,1)S(1)}, u32[]{:S(2)}, u32[]{:S(2)}) collective-permute-start(bf16[1,400,256]{2,1,0:T(8,128)(2,1)S(1)} %slice.146), channel_id=1, source_target_pairs={{0,4},{1,5},{2,6},{3,7},{4,8},{5,9},{6,10},{7,11},{8,12},{9,13},{1... | collective-permute-start | bytes 614408 | tf_op jit(solution)/shard_map/ppermute | solution.py:30
  135.5 6.9 %collective-permute-start.36 = (bf16[1,400,256]{2,1,0:T(8,128)(2,1)S(1)}, bf16[1,400,256]{2,1,0:T(8,128)(2,1)S(1)}, u32[]{:S(2)}, u32[]{:S(2)}) collective-permute-start(bf16[1,400,256]{2,1,0:T(8,128)(2,1)S(1)} %slice.149), channel_id=1, source_target_pairs={{0,12},{1,13},{2,14},{3,15},{4,0},{5,1},{6,2},{7,3},{8,4},{9,5},{1... | collective-permute-start | bytes 614408 | tf_op jit(solution)/shard_map/ppermute | solution.py:30
  143.6 7.7 %collective-permute-start.40 = (bf16[1,512,256]{2,1,0:T(8,128)(2,1)S(1)}, bf16[1,512,256]{2,1,0:T(8,128)(2,1)S(1)}, u32[]{:S(2)}, u32[]{:S(2)}) collective-permute-start(bf16[1,512,256]{2,1,0:T(8,128)(2,1)S(1)} %get-tuple-element.117), channel_id=1, source_target_pairs={{0,16},{1,17},{2,18},{3,19},{4,20},{5,21},{6,22},{7,23},{8,24},{9,... | collective-permute-start | bytes 786440 | tf_op jit(solution)/shard_map/ppermute | solution.py:30
  143.7 7.6 %collective-permute-start.41 = (bf16[1,512,256]{2,1,0:T(8,128)(2,1)S(1)}, bf16[1,512,256]{2,1,0:T(8,128)(2,1)S(1)}, u32[]{:S(2)}, u32[]{:S(2)}) collective-permute-start(bf16[1,512,256]{2,1,0:T(8,128)(2,1)S(1)} %get-tuple-element.116), channel_id=1, source_target_pairs={{0,48},{1,49},{2,50},{3,51},{4,52},{5,53},{6,54},{7,55},{8,56},{9,... | collective-permute-start | bytes 786440 | tf_op jit(solution)/shard_map/ppermute | solution.py:30
  151.5 10.5 %collective-permute-start.42 = (bf16[2,512,256]{2,1,0:T(8,128)(2,1)S(1)}, bf16[2,512,256]{2,1,0:T(8,128)(2,1)S(1)}, u32[]{:S(2)}, u32[]{:S(2)}) collective-permute-start(bf16[2,512,256]{2,1,0:T(8,128)(2,1)S(1)} %pad_maximum_fusion.6), channel_id=1, source_target_pairs={{0,16},{1,17},{2,18},{3,19},{4,20},{5,21},{6,22},{7,23},{8,24},{9,... | collective-permute-start | bytes 1572872 | tf_op jit(solution)/shard_map/ppermute | solution.py:30
  153.0 9.3 %collective-permute-start.43 = (bf16[2,512,256]{2,1,0:T(8,128)(2,1)S(1)}, bf16[2,512,256]{2,1,0:T(8,128)(2,1)S(1)}, u32[]{:S(2)}, u32[]{:S(2)}) collective-permute-start(bf16[2,512,256]{2,1,0:T(8,128)(2,1)S(1)} %pad_maximum_fusion.7), channel_id=1, source_target_pairs={{0,48},{1,49},{2,50},{3,51},{4,52},{5,53},{6,54},{7,55},{8,56},{9,... | collective-permute-start | bytes 1572872 | tf_op jit(solution)/shard_map/ppermute | solution.py:30
  155.0 8.1 %collective-permute-start.39 = (bf16[512,256]{1,0:T(8,128)(2,1)S(1)}, bf16[512,256]{1,0:T(8,128)(2,1)S(1)}, u32[]{:S(2)}, u32[]{:S(2)}) collective-permute-start(bf16[512,256]{1,0:T(8,128)(2,1)S(1)} %fusion.4), channel_id=1, source_target_pairs={{0,64},{1,65},{2,66},{3,67},{4,68},{5,69},{6,70},{7,71},{8,72},{9,... | collective-permute-start | bytes 786440 | tf_op jit(solution)/shard_map/ppermute | solution.py:30
  162.5 6.5 %collective-permute-start.44 = (bf16[512,256]{1,0:T(8,128)(2,1)S(1)}, bf16[512,256]{1,0:T(8,128)(2,1)S(1)}, u32[]{:S(2)}, u32[]{:S(2)}) collective-permute-start(bf16[512,256]{1,0:T(8,128)(2,1)S(1)} %fusion.5), channel_id=1, source_target_pairs={{0,64},{1,65},{2,66},{3,67},{4,68},{5,69},{6,70},{7,71},{8,72},{9,... | collective-permute-start | bytes 786440 | tf_op jit(solution)/shard_map/ppermute | solution.py:30
  (6 other events, 5.7 us)
